TPU v7x, 256 devices: a whole 4x4x8 slice. The times are simulated.
256 devices in a mesh: blk: 32 (over z, x_lo, core), hd: 8 (over x_hi, y).
Axes of the slice: x: 4 (x_hi: 2, x_lo: 2; x = x_hi * 2 + x_lo), y: 4, z: 8, core: 2. Of those that a mesh axis runs over, the one named last changes fastest.
Arguments:
- queries: bfloat16 [16384, 4096], P(('blk', 'hd')), may hold values from -8 to 8
- keys: bfloat16 [16384, 1024], P(('blk', 'hd')), may hold values from -8 to 8
- values: bfloat16 [16384, 1024], P(('blk', 'hd')), may hold values from -6 to 6
Outputs:
- attended: bfloat16 [16384, 4096], P(('blk', 'hd'))
All inputs are finite; a program needn't handle non-finite values.
Results may differ from a plain program's by a relative error of at most 0.0044.
Values may be sent and summed in bfloat16 or wider, within the bound.
No kernel may reach another device: no remote copies, remote signals or barrier semaphores. Data moves between devices by JAX's collectives and lax.ppermute only.
A program may use at most 64 MiB of HBM per device.

v0:
```python
import jax
import jax.numpy as jnp
from jax import lax
from jax.sharding import PartitionSpec as P

H = 32
KV = 8
HD = 128
BLK = 256


def broadcast(array, axis, root):
    mine = lax.axis_index(axis) == root
    return lax.psum(jnp.where(mine, array, jnp.zeros_like(array)), axis)


def head_attention(query_part, key_part, value_part, visible, scaling):
    scores = (
        jnp.einsum("qd,kd->qk", query_part, key_part, preferred_element_type=jnp.float32) * scaling
    )
    masked = jnp.where(visible, scores, -jnp.inf)
    largest = jnp.max(masked, axis=1, keepdims=True)
    raised = jnp.exp(masked - largest)
    totals = jnp.sum(raised, axis=1, keepdims=True)
    weights = raised.astype(jnp.bfloat16)
    mixture = jnp.dot(weights, value_part, preferred_element_type=jnp.float32)
    return (mixture / totals).astype(jnp.bfloat16)


def shards(queries, keys, values):
    scaling = HD ** (-0.5)
    query_heads, key_heads, value_heads = (
        lax.all_to_all(queries, "hd", split_axis=1, concat_axis=0, tiled=True),
        lax.all_to_all(keys, "hd", split_axis=1, concat_axis=0, tiled=True),
        lax.all_to_all(values, "hd", split_axis=1, concat_axis=0, tiled=True),
    )
    anchor_keys, anchor_values = (
        broadcast(key_heads[:BLK], "blk", 0),
        broadcast(value_heads[:BLK], "blk", 0),
    )
    heads_here = query_heads.shape[1] // HD
    group_size = H // KV
    group_index = lax.axis_index("blk")
    positions = jnp.arange(BLK)[:, None]
    columns = jnp.arange(2 * BLK)[None, :]
    pieces = []
    for block_slot in range(2):
        anchored = 2 * group_index + block_slot > 0
        visible = jnp.where(columns < BLK, anchored, columns - BLK <= positions)
        start = block_slot * BLK
        head_outputs = []
        for head_slot in range(heads_here):
            kv_slot = head_slot // group_size
            query_part = query_heads[start : start + BLK, head_slot * HD : (head_slot + 1) * HD]
            key_part = jnp.concatenate(
                [anchor_keys, key_heads[start : start + BLK, kv_slot * HD : (kv_slot + 1) * HD]],
                axis=0,
            )
            value_part = jnp.concatenate(
                [
                    anchor_values,
                    value_heads[start : start + BLK, kv_slot * HD : (kv_slot + 1) * HD],
                ],
                axis=0,
            )
            head_outputs.append(head_attention(query_part, key_part, value_part, visible, scaling))
        pieces.append(jnp.concatenate(head_outputs, axis=1))
    attended = jnp.concatenate(pieces, axis=0)
    return lax.all_to_all(attended, "hd", split_axis=0, concat_axis=1, tiled=True)


def solution(mesh):
    placed = (P(("blk", "hd"), None), P(("blk", "hd"), None), P(("blk", "hd"), None))
    return jax.shard_map(
        shards, mesh=mesh, in_specs=placed, out_specs=P(("blk", "hd"), None), check_vma=False
    )
```

profile of v0, /device:TPU:1, one launch (start us, length us, event | category | flops | bytes accessed | tf_op | source)
XLA Modules:
  0.0 277.2 jit_solution(4570407309087471163)
XLA Ops:
  6.5 0.9 copy-done
  7.4 0.7 copy_bitcast_fusion.2
  8.1 7.5 %all-to-all-start = ((bf16[64,8,128]{2,0,1:T(8,128)(2,1)}), bf16[64,8,128]{2,0,1:T(8,128)(2,1)S(1)}, u32[]{:S(2)}, u32[]{:S(2)}) async-start(bf16[64,8,128]{2,0,1:T(8,128)(2,1)} %copy_bitcast_fusion.2), calls=%async_computation | async-start | bytes 262144 | tf_op jit(solution)/shard_map/all_to_all | solution.py:34
  15.6 1.6 copy_bitcast_fusion.1
  17.2 0.8 copy.25
  18.0 4.5 %all-to-all-done = bf16[64,8,128]{2,0,1:T(8,128)(2,1)S(1)} async-done(((bf16[64,8,128]{2,0,1:T(8,128)(2,1)}), bf16[64,8,128]{2,0,1:T(8,128)(2,1)S(1)}, u32[]{:S(2)}, u32[]{:S(2)}) %all-to-all-start) | async-done | bytes 131104 | tf_op jit(solution)/shard_map/all_to_all | solution.py:34
  22.5 3.4 %all-to-all-start.2 = ((bf16[64,8,128]{2,0,1:T(8,128)(2,1)}), bf16[64,8,128]{2,0,1:T(8,128)(2,1)S(1)}, u32[]{:S(2)}, u32[]{:S(2)}) async-start(bf16[64,8,128]{2,0,1:T(8,128)(2,1)} %copy_bitcast_fusion.1), calls=%async_computation.2 | async-start | bytes 262144 | tf_op jit(solution)/shard_map/all_to_all | solution.py:35
  25.9 7.0 %all-to-all-done.2 = bf16[64,8,128]{2,0,1:T(8,128)(2,1)S(1)} async-done(((bf16[64,8,128]{2,0,1:T(8,128)(2,1)}), bf16[64,8,128]{2,0,1:T(8,128)(2,1)S(1)}, u32[]{:S(2)}, u32[]{:S(2)}) %all-to-all-start.2) | async-done | bytes 131104 | tf_op jit(solution)/shard_map/all_to_all | solution.py:35
  32.9 3.5 %all-to-all-start.1 = ((bf16[64,8,512]{2,0,1:T(8,128)(2,1)}), bf16[64,8,512]{2,0,1:T(8,128)(2,1)S(1)}, u32[]{:S(2)}, u32[]{:S(2)}) async-start(bf16[64,8,512]{2,0,1:T(8,128)(2,1)} %bitcast.60), calls=%async_computation.1 | async-start | bytes 1048576 | tf_op jit(solution)/shard_map/all_to_all | solution.py:33
  36.5 0.7 broadcast_select_fusion
  37.2 210.0 %all-reduce.3.cloned.1.call-done = (bf16[256,128]{1,0:T(8,128)(2,1)}, bf16[256,128]{1,0:T(8,128)(2,1)}) async-done(((bf16[256,128]{1,0:T(8,128)(2,1)}, bf16[256,128]{1,0:T(8,128)(2,1)}), (bf16[256,128]{1,0:T(8,128)(2,1)}, bf16[256,128]{1,0:T(8,128)(2,1)})) %all-reduce.3.cloned.1.call-update) | async-done | bytes 131088 | tf_op jit(solution)/shard_map/psum | solution.py:14
  247.3 1.2 fusion.75
  248.5 0.3 fusion.74
  248.8 0.3 fusion.73
  249.1 0.3 fusion.72
  249.4 0.3 fusion.71
  249.6 0.3 fusion.70
  249.9 0.3 fusion.69
  250.2 0.3 fusion.68
  250.8 0.7 copy-done.2
  251.7 0.2 fusion.17
  252.1 0.2 fusion.18
  254.5 15.0 %all_to_all.70 = bf16[8,64,512]{2,1,0:T(8,128)(2,1)S(1)} all-to-all(bf16[8,64,512]{2,1,0:T(8,128)(2,1)S(1)} %bitcast.61), channel_id=1, replica_groups=mesh['blk'=32,'hd'=8] {'hd'}, dimensions={0} | all-to-all | bytes 1048576 | tf_op jit(solution)/shard_map/all_to_all | solution.py:69
  269.5 0.8 copy.21
  (29 shorter events, 2.8 us)
Async XLA Ops:
  6.5 0.9 copy-start
  7.4 9.7 %copy-start.1 = (bf16[64,4096]{1,0:T(8,128)(2,1)S(1)}, bf16[64,4096]{1,0:T(8,128)(2,1)}, u32[]{:S(2)}) copy-start(bf16[64,4096]{1,0:T(8,128)(2,1)} %param.3) | copy-start | bytes 1572868
  8.1 14.4 %all-to-all-start = ((bf16[64,8,128]{2,0,1:T(8,128)(2,1)}), bf16[64,8,128]{2,0,1:T(8,128)(2,1)S(1)}, u32[]{:S(2)}, u32[]{:S(2)}) async-start(bf16[64,8,128]{2,0,1:T(8,128)(2,1)} %copy_bitcast_fusion.2), calls=%async_computation | async-start | bytes 262144 | tf_op jit(solution)/shard_map/all_to_all | solution.py:34
  22.5 10.4 %all-to-all-start.2 = ((bf16[64,8,128]{2,0,1:T(8,128)(2,1)}), bf16[64,8,128]{2,0,1:T(8,128)(2,1)S(1)}, u32[]{:S(2)}, u32[]{:S(2)}) async-start(bf16[64,8,128]{2,0,1:T(8,128)(2,1)} %copy_bitcast_fusion.1), calls=%async_computation.2 | async-start | bytes 262144 | tf_op jit(solution)/shard_map/all_to_all | solution.py:35
  32.9 214.4 %all-to-all-start.1 = ((bf16[64,8,512]{2,0,1:T(8,128)(2,1)}), bf16[64,8,512]{2,0,1:T(8,128)(2,1)S(1)}, u32[]{:S(2)}, u32[]{:S(2)}) async-start(bf16[64,8,512]{2,0,1:T(8,128)(2,1)} %bitcast.60), calls=%async_computation.1 | async-start | bytes 1048576 | tf_op jit(solution)/shard_map/all_to_all | solution.py:33
  36.4 210.8 %all-reduce.3.cloned.1.call-start = ((), (), s32[]{:S(2)}) async-start(), calls=%async_computation.4 | async-start | bytes 262144 | tf_op jit(solution)/shard_map/psum | solution.py:14
  247.3 1.2 copy-start.3
  250.6 0.8 copy-start.2
Sparse Core Ops, SparseCore 0:
  40.0 207.2 all-reduce.2
where the time goes:
time: 279 us; the launch traced here: 277 us
  waiting for transfers between devices  222 us (80%)
  blocking collectives  15 us (5%)
  starting transfers between devices  14.4 us (5%)
  between operations  13.6 us (5%)
  local copies, waits for them, and re-layouts  5.79 us (2%)
  matrix products  5.18 us (2%)
    psum x1, waiting for transfers between devices, broadcast(): return lax.psum(jnp.where(mine, array, jnp.zeros_like(array)), axis)  210 us
    all_to_all x1, blocking collectives, shards(): lax.all_to_all(attended, 'hd', split_axis=0, concat_axis=1, tiled=True)  15 us
    all_to_all x1, starting transfers between devices, shards(): lax.all_to_all(keys, 'hd', split_axis=1, concat_axis=0, tiled=True)  7.48 us
    all_to_all x1, waiting for transfers between devices, shards(): lax.all_to_all(values, 'hd', split_axis=1, concat_axis=0, tiled=True)  7 us
  transfers between devices with their start and end apart: 4, of which 3 were waited for; matrix products, arithmetic and copies ran while one was open for 1% of the time, Pallas kernels for 0%

commit v1 on v0

v1 whole, which is shorter than its diff:
```python
import functools

import jax
import jax.numpy as jnp
import numpy as np
from jax import lax
from jax.experimental import pallas as pl
from jax.experimental.pallas import tpu as pltpu
from jax.sharding import PartitionSpec as P

H = 32
KV = 8
HD = 128
BLK = 256
ROWS = 64
GROUP = H // KV
HALF = KV // 2
RATE = HD ** (-0.5) * 1.4426950408889634
AXES = ("blk", "hd")


def place(x, y, z, core):
    return (z * 4 + (x % 2) * 2 + core) * 8 + (x // 2) * 4 + y


def whereabouts():
    blk, hd = lax.axis_index("blk"), lax.axis_index("hd")
    return (hd >> 2) * 2 + ((blk >> 1) & 1), hd & 3, blk >> 2, blk & 1


def on_chips(chips):
    x, _, z, _ = whereabouts()
    bits = 0
    for a, b in chips:
        bits |= 1 << (a * 8 + b)
    shift = (x * 8 + z).astype(jnp.uint32)
    return ((jnp.uint32(np.uint32(bits)) >> shift) & 1) == 1


def along_y(array, step, wrap):
    pairs = [
        (place(x, y, z, core), place(x, (y + step) % 4, z, core))
        for x in range(4)
        for y in range(4)
        for z in range(8)
        for core in range(2)
        if wrap or y + step < 4
    ]
    return lax.ppermute(array, AXES, pairs)


LEVELS = (((1, 0), (3, 0), (2, 0)), ((0, 2), (0, 6), (0, 4)), ((0, 1),))


def spread(piece, beside):
    have = [(0, 0)]
    for number, level in enumerate(LEVELS):
        came = []
        for dx, dz in level:
            moves = [((x, z), ((x + dx) % 4, (z + dz) % 8)) for x, z in have]
            pairs = [
                (place(a[0], y, a[1], core), place(b[0], y, b[1], core))
                for a, b in moves
                for y in range(4)
                for core in range(2)
            ]
            came.append((lax.ppermute(piece, AXES, pairs), [b for _, b in moves]))
        if number == len(LEVELS) - 1:
            (got, chips), = came
            got, beside = lax.optimization_barrier((got, beside))
            came = [(got, chips)]
        for got, chips in came:
            piece = jnp.where(on_chips(chips), got, piece)
            have = have + chips
    return piece, beside


def stacked_queries(q_ref, g):
    return jnp.concatenate(
        [q_ref[:, (g * GROUP + i) * HD : (g * GROUP + i + 1) * HD] for i in range(GROUP)], axis=0
    )


def raw_scores(query, key):
    return lax.dot_general(query, key, (((1,), (1,)), ((), ())), preferred_element_type=jnp.float32)


def own_kernel(q_ref, own_ref, one_ref, two_ref, three_ref, mix_ref, stat_ref):
    y = lax.axis_index("hd") & 3
    rows = GROUP * ROWS
    row = lax.broadcasted_iota(jnp.int32, (rows, BLK), 0) & (ROWS - 1)
    column = lax.broadcasted_iota(jnp.int32, (rows, BLK), 1)
    visible = column <= jnp.where(column < ROWS, row, y * ROWS + ROWS - 1)
    refs = (own_ref, one_ref, two_ref, three_ref)
    for g in range(KV):
        base = (g // HALF) * 2 * HALF * HD + (g % HALF) * HD
        key = jnp.concatenate([r[:, base : base + HD] for r in refs], axis=0)
        value = jnp.concatenate(
            [r[:, base + HALF * HD : base + HALF * HD + HD] for r in refs], axis=0
        )
        masked = jnp.where(visible, raw_scores(stacked_queries(q_ref, g), key), -jnp.inf)
        largest = jnp.max(masked, axis=1, keepdims=True)
        raised = jnp.exp2((masked - largest) * RATE)
        totals = jnp.sum(raised, axis=1, keepdims=True)
        mix_ref[g] = jnp.dot(
            raised.astype(jnp.bfloat16), value, preferred_element_type=jnp.float32
        )
        stat_ref[g] = jnp.where(
            lax.broadcasted_iota(jnp.int32, (rows, HD), 1) < 64, largest, totals
        )


def own_attention(queries, pieces):
    rows = GROUP * ROWS
    return pl.pallas_call(
        own_kernel,
        out_shape=(
            jax.ShapeDtypeStruct((KV, rows, HD), jnp.float32),
            jax.ShapeDtypeStruct((KV, rows, HD), jnp.float32),
        ),
        cost_estimate=pl.CostEstimate(
            flops=4 * KV * rows * BLK * HD, bytes_accessed=4 << 20, transcendentals=KV * rows * BLK
        ),
        compiler_params=pltpu.CompilerParams(vmem_limit_bytes=32 << 20),
        name="own_attention",
    )(queries, *pieces)


def anchor_kernel(first, q_ref, mix_ref, stat_ref, a0, a1, a2, a3, b_ref, out_ref):
    blk, hd = lax.axis_index("blk"), lax.axis_index("hd")
    anchored = blk * 2 + (hd >> 2) > 0
    swap = (blk & 1) == 1
    mine = (a0, a1, a2, a3)

    def head(g, key, value):
        scores = jnp.where(anchored, raw_scores(stacked_queries(q_ref, g), key), -jnp.inf)
        old = stat_ref[g][:, 0:1]
        old_totals = stat_ref[g][:, 64:65]
        largest = jnp.maximum(jnp.max(scores, axis=1, keepdims=True), old)
        raised = jnp.exp2((scores - largest) * RATE)
        keep = jnp.exp2((old - largest) * RATE)
        totals = jnp.sum(raised, axis=1, keepdims=True) + old_totals * keep
        mixture = (
            jnp.dot(raised.astype(jnp.bfloat16), value, preferred_element_type=jnp.float32)
            + mix_ref[g] * keep
        )
        result = (mixture / totals).astype(jnp.bfloat16)
        for i in range(GROUP):
            out_ref[:, (g * GROUP + i) * HD : (g * GROUP + i + 1) * HD] = result[
                i * ROWS : (i + 1) * ROWS
            ]

    for g in range(KV):
        column = (g % HALF) * HD
        here = swap == (g >= HALF)
        parts = []
        for offset in (column, column + HALF * HD):
            near = jnp.concatenate([r[:, offset : offset + HD] for r in mine], axis=0)
            parts.append(jnp.where(here, near, b_ref[:, offset : offset + HD]))
        head(g, *parts)


def anchor_attention(queries, mixture, stats, mine, other):
    rows = GROUP * ROWS
    return pl.pallas_call(
        functools.partial(anchor_kernel, True),
        out_shape=jax.ShapeDtypeStruct((ROWS, H * HD), jnp.bfloat16),
        cost_estimate=pl.CostEstimate(
            flops=4 * KV * rows * BLK * HD, bytes_accessed=4 << 20, transcendentals=KV * rows * BLK
        ),
        compiler_params=pltpu.CompilerParams(vmem_limit_bytes=32 << 20),
        name="anchor_attention",
    )(queries, mixture, stats, *mine, other)


def shards(queries, keys, values):
    _, _, _, core = whereabouts()
    width = HALF * HD
    low = jnp.concatenate([keys[:, :width], values[:, :width]], axis=1)
    high = jnp.concatenate([keys[:, width:], values[:, width:]], axis=1)
    both = jnp.concatenate([low, high], axis=1)
    across = lax.ppermute(high, AXES, [(place(0, y, 0, 0), place(0, y, 0, 1)) for y in range(4)])
    pieces = [both] + [along_y(both, step, False) for step in (1, 2, 3)]
    anchor, (mixture, stats) = spread(
        jnp.where(core == 1, across, low), own_attention(queries, pieces)
    )
    mine = [anchor] + [along_y(anchor, step, True) for step in (1, 3, 2)]
    swaps = [(place(x, y, z, c), place(x, y, z, 1 - c)) for x in range(4) for y in range(4) for z in range(8) for c in range(2)]
    other = lax.ppermute(jnp.concatenate(mine, axis=0), AXES, swaps)
    return anchor_attention(queries, mixture, stats, mine, other)


def solution(mesh):
    rows = P(("blk", "hd"), None)
    return jax.shard_map(
        shards, mesh=mesh, in_specs=(rows, rows, rows), out_specs=rows, check_vma=False
    )
```

time: 279 us -> 53.6 us (0.19)
  waiting for transfers between devices: 222 us -> 19 us
  blocking collectives: 15 us -> 0 us
  between operations: 13.6 us -> 0.22 us
  starting transfers between devices: 14.4 us -> 26.7 us
  Pallas kernels: 0 us -> 6.16 us
  matrix products: 5.18 us -> 0 us
  local copies, waits for them, and re-layouts: 5.79 us -> 0.96 us
    psum x1 -> x0, waiting for transfers between devices: 210 us -> none  [broadcast(): return lax.psum(jnp.where(mine, array, jnp.zeros_like(array)), axis)]
    ppermute x0 -> x15, starting transfers between devices: none -> 26.7 us  [the longest x6 13.3 us: along_y(): return lax.ppermute(array, AXES, pairs)]
    ppermute x0 -> x15, waiting for transfers between devices: none -> 19 us  [the longest x6 10 us: along_y(): return lax.ppermute(array, AXES, pairs)]
    all_to_all x1 -> x0, blocking collectives: 15 us -> none  [shards(): lax.all_to_all(attended, 'hd', split_axis=0, concat_axis=1, tiled=True)]
    all_to_all x3 -> x0, starting transfers between devices: 14.3 us -> none  [the longest x1 7.48 us: shards(): lax.all_to_all(keys, 'hd', split_axis=1, concat_axis=0, tiled=True)]
    all_to_all x3 -> x0, waiting for transfers between devices: 11.5 us -> none  [the longest x1 7 us: shards(): lax.all_to_all(values, 'hd', split_axis=1, concat_axis=0, tiled=True)]
    pallas_call x0 -> x2, Pallas kernels: none -> 6.16 us  [the longest x1 5.04 us: anchor_attention(): pl.pallas_call(functools.partial(anchor_kernel, True), out_shape=jax.Shap...]
    dot_general x16 -> x0, matrix products: 5.18 us -> none  [the longest x8 3.2 us: head_attention(): jnp.einsum('qd,kd->qk', query_part, key_part, preferred_element_type=jnp....]
  transfers between devices with their start and end apart: 4 -> 15, of which waited for: 3 -> 10; matrix products, arithmetic and copies ran while one was open for 1% -> 0% of each run, Pallas kernels for 0% -> 2%
where the time goes in v1:
time: 53.6 us; the launch traced here: 53.2 us
  starting transfers between devices  26.7 us (50%)
  waiting for transfers between devices  19 us (35%)
  Pallas kernels  6.16 us (11%)
  local copies, waits for them, and re-layouts  0.96 us (2%)
    ppermute x6, starting transfers between devices, along_y(): return lax.ppermute(array, AXES, pairs)  13.3 us
    ppermute x6, waiting for transfers between devices, along_y(): return lax.ppermute(array, AXES, pairs)  10 us
    ppermute x7, starting transfers between devices, spread(): came.append((lax.ppermute(piece, AXES, pairs), [b for _, b in moves]))  9.21 us
    pallas_call x1, Pallas kernels, anchor_attention(): pl.pallas_call(functools.partial(anchor_kernel, True), out_shape=jax.Shap...  5.04 us
    ppermute x1, waiting for transfers between devices, shards(): lax.ppermute(high, AXES, [(place(0, y, 0, 0), place(0, y, 0, 1)) for y in...  4.05 us
    ppermute x7, waiting for transfers between devices, spread(): came.append((lax.ppermute(piece, AXES, pairs), [b for _, b in moves]))  3.35 us
    ppermute x1, starting transfers between devices, shards(): other = lax.ppermute(jnp.concatenate(mine, axis=0), AXES, swaps)  2.84 us
    ppermute x1, waiting for transfers between devices, shards(): other = lax.ppermute(jnp.concatenate(mine, axis=0), AXES, swaps)  1.54 us
  transfers between devices with their start and end apart: 15, of which 10 were waited for; matrix products, arithmetic and copies ran while one was open for 0% of the time, Pallas kernels for 2%

profile of v1, /device:TPU:1, one launch (start us, length us, event | category | flops | bytes accessed | tf_op | source)
XLA Modules:
  0.0 53.2 jit_solution(11412143856431498481)
XLA Ops:
  1.0 1.3 %collective-permute-start = (bf16[64,1024]{1,0:T(8,128)(2,1)S(1)}, bf16[64,1024]{1,0:T(8,128)(2,1)S(1)}, u32[]{:S(2)}, u32[]{:S(2)}) collective-permute-start(bf16[64,1024]{1,0:T(8,128)(2,1)S(1)} %pad_maximum_fusion.2), channel_id=1, source_target_pairs={{0,8},{1,9},{2,10},{3,11}} | collective-permute-start | bytes 393224 | tf_op jit(solution)/shard_map/ppermute | solution.py:182
  2.3 4.1 %collective-permute-done = bf16[64,1024]{1,0:T(8,128)(2,1)S(1)} collective-permute-done((bf16[64,1024]{1,0:T(8,128)(2,1)S(1)}, bf16[64,1024]{1,0:T(8,128)(2,1)S(1)}, u32[]{:S(2)}, u32[]{:S(2)}) %collective-permute-start) | collective-permute-done | bytes 131104 | tf_op jit(solution)/shard_map/ppermute | solution.py:182
  6.4 1.3 %collective-permute-start.3 = (bf16[64,1024]{1,0:T(8,128)(2,1)S(1)}, bf16[64,1024]{1,0:T(8,128)(2,1)S(1)}, u32[]{:S(2)}, u32[]{:S(2)}) collective-permute-start(bf16[64,1024]{1,0:T(8,128)(2,1)S(1)} %maximum_select_fusion), channel_id=1, source_target_pairs={{0,16},{8,24},{1,17},{9,25},{2,18},{10,26},{3,19},{11,27}} | collective-permute-start | bytes 393224 | tf_op jit(solution)/shard_map/ppermute | solution.py:67
  7.7 1.3 %collective-permute-start.2 = (bf16[64,1024]{1,0:T(8,128)(2,1)S(1)}, bf16[64,1024]{1,0:T(8,128)(2,1)S(1)}, u32[]{:S(2)}, u32[]{:S(2)}) collective-permute-start(bf16[64,1024]{1,0:T(8,128)(2,1)S(1)} %maximum_select_fusion), channel_id=1, source_target_pairs={{0,20},{8,28},{1,21},{9,29},{2,22},{10,30},{3,23},{11,31}} | collective-permute-start | bytes 393224 | tf_op jit(solution)/shard_map/ppermute | solution.py:67
  9.0 1.3 %collective-permute-start.1 = (bf16[64,1024]{1,0:T(8,128)(2,1)S(1)}, bf16[64,1024]{1,0:T(8,128)(2,1)S(1)}, u32[]{:S(2)}, u32[]{:S(2)}) collective-permute-start(bf16[64,1024]{1,0:T(8,128)(2,1)S(1)} %maximum_select_fusion), channel_id=1, source_target_pairs={{0,4},{8,12},{1,5},{9,13},{2,6},{10,14},{3,7},{11,15}} | collective-permute-start | bytes 393224 | tf_op jit(solution)/shard_map/ppermute | solution.py:67
  10.6 1.3 %collective-permute-done.2 = bf16[64,1024]{1,0:T(8,128)(2,1)S(1)} collective-permute-done((bf16[64,1024]{1,0:T(8,128)(2,1)S(1)}, bf16[64,1024]{1,0:T(8,128)(2,1)S(1)}, u32[]{:S(2)}, u32[]{:S(2)}) %collective-permute-start.2) | collective-permute-done | bytes 131104 | tf_op jit(solution)/shard_map/ppermute | solution.py:67
  11.9 1.7 %collective-permute-done.1 = bf16[64,1024]{1,0:T(8,128)(2,1)S(1)} collective-permute-done((bf16[64,1024]{1,0:T(8,128)(2,1)S(1)}, bf16[64,1024]{1,0:T(8,128)(2,1)S(1)}, u32[]{:S(2)}, u32[]{:S(2)}) %collective-permute-start.1) | collective-permute-done | bytes 131104 | tf_op jit(solution)/shard_map/ppermute | solution.py:67
  13.7 1.4 %collective-permute-start.6 = (bf16[64,1024]{1,0:T(8,128)(2,1)S(1)}, bf16[64,1024]{1,0:T(8,128)(2,1)S(1)}, u32[]{:S(2)}, u32[]{:S(2)}) collective-permute-start(bf16[64,1024]{1,0:T(8,128)(2,1)S(1)} %select_select_fusion.1), channel_id=1, source_target_pairs={{0,64},{8,72},{1,65},{9,73},{2,66},{10,74},{3,67},{11,75},{16,80},... | collective-permute-start | bytes 393224 | tf_op jit(solution)/shard_map/ppermute | solution.py:67
  15.1 1.3 %collective-permute-start.5 = (bf16[64,1024]{1,0:T(8,128)(2,1)S(1)}, bf16[64,1024]{1,0:T(8,128)(2,1)S(1)}, u32[]{:S(2)}, u32[]{:S(2)}) collective-permute-start(bf16[64,1024]{1,0:T(8,128)(2,1)S(1)} %select_select_fusion.1), channel_id=1, source_target_pairs={{0,192},{8,200},{1,193},{9,201},{2,194},{10,202},{3,195},{11,203},... | collective-permute-start | bytes 393224 | tf_op jit(solution)/shard_map/ppermute | solution.py:67
  16.4 1.3 %collective-permute-start.4 = (bf16[64,1024]{1,0:T(8,128)(2,1)S(1)}, bf16[64,1024]{1,0:T(8,128)(2,1)S(1)}, u32[]{:S(2)}, u32[]{:S(2)}) collective-permute-start(bf16[64,1024]{1,0:T(8,128)(2,1)S(1)} %select_select_fusion.1), channel_id=1, source_target_pairs={{0,128},{8,136},{1,129},{9,137},{2,130},{10,138},{3,131},{11,139},... | collective-permute-start | bytes 393224 | tf_op jit(solution)/shard_map/ppermute | solution.py:67
  17.8 2.6 %collective-permute-start.10 = (bf16[64,2048]{1,0:T(8,128)(2,1)S(1)}, bf16[64,2048]{1,0:T(8,128)(2,1)S(1)}, u32[]{:S(2)}, u32[]{:S(2)}) collective-permute-start(bf16[64,2048]{1,0:T(8,128)(2,1)S(1)} %pad_maximum_fusion.1.own_ref), channel_id=1, source_target_pairs={{0,3},{8,11},{32,35},{40,43},{64,67},{72,75},{96,99},{104,107},{12... | collective-permute-start | bytes 786440 | tf_op jit(solution)/shard_map/ppermute | solution.py:49
  20.4 1.3 %collective-permute-start.9 = (bf16[64,2048]{1,0:T(8,128)(2,1)S(1)}, bf16[64,2048]{1,0:T(8,128)(2,1)S(1)}, u32[]{:S(2)}, u32[]{:S(2)}) collective-permute-start(bf16[64,2048]{1,0:T(8,128)(2,1)S(1)} %pad_maximum_fusion.1.own_ref), channel_id=1, source_target_pairs={{0,2},{8,10},{32,34},{40,42},{64,66},{72,74},{96,98},{104,106},{12... | collective-permute-start | bytes 786440 | tf_op jit(solution)/shard_map/ppermute | solution.py:49
  21.7 2.5 %collective-permute-start.8 = (bf16[64,2048]{1,0:T(8,128)(2,1)S(1)}, bf16[64,2048]{1,0:T(8,128)(2,1)S(1)}, u32[]{:S(2)}, u32[]{:S(2)}) collective-permute-start(bf16[64,2048]{1,0:T(8,128)(2,1)S(1)} %pad_maximum_fusion.1.own_ref), channel_id=1, source_target_pairs={{0,1},{8,9},{32,33},{40,41},{64,65},{72,73},{96,97},{104,105},{128... | collective-permute-start | bytes 786440 | tf_op jit(solution)/shard_map/ppermute | solution.py:49
  24.3 1.3 %collective-permute-start.7 = (bf16[64,1024]{1,0:T(8,128)(2,1)S(1)}, bf16[64,1024]{1,0:T(8,128)(2,1)S(1)}, u32[]{:S(2)}, u32[]{:S(2)}) collective-permute-start(bf16[64,1024]{1,0:T(8,128)(2,1)S(1)} %select_select_fusion), channel_id=1, source_target_pairs={{0,32},{8,40},{1,33},{9,41},{2,34},{10,42},{3,35},{11,43},{16,48},... | collective-permute-start | bytes 393224 | tf_op jit(solution)/shard_map/ppermute | solution.py:67
  25.6 4.8 %collective-permute-done.10.three_ref = bf16[64,2048]{1,0:T(8,128)(2,1)S(1)} collective-permute-done((bf16[64,2048]{1,0:T(8,128)(2,1)S(1)}, bf16[64,2048]{1,0:T(8,128)(2,1)S(1)}, u32[]{:S(2)}, u32[]{:S(2)}) %collective-permute-start.10) | collective-permute-done | bytes 262176 | tf_op jit(solution)/shard_map/ppermute | solution.py:49
  30.4 1.3 %collective-permute-done.8.one_ref = bf16[64,2048]{1,0:T(8,128)(2,1)S(1)} collective-permute-done((bf16[64,2048]{1,0:T(8,128)(2,1)S(1)}, bf16[64,2048]{1,0:T(8,128)(2,1)S(1)}, u32[]{:S(2)}, u32[]{:S(2)}) %collective-permute-start.8) | collective-permute-done | bytes 262176 | tf_op jit(solution)/shard_map/ppermute | solution.py:49
  31.7 1.1 %own_attention.1 = (f32[8,256,128]{2,1,0:T(8,128)S(1)}, f32[8,256,128]{2,1,0:T(8,128)S(1)}) custom-call(bf16[64,4096]{1,0:T(8,128)(2,1)S(1)} %copy-done, bf16[64,2048]{1,0:T(8,128)(2,1)S(1)} %pad_maximum_fusion.1.own_ref, bf16[64,2048]{1,0:T(8,128)(2,1)S(1)} %collective-permute-done.8.one_ref, bf16[64,2048]{1,0:T(8,128)(2,1)S(1)} %collective-permute-done.9.two_ref, ...), custom_call_target="tpu_custom_call" | custom-call | flops 268435456 | bytes 4194304 | tf_op jit(solution)/shard_map/own_attention/pallas_call | solution.py:115
  32.9 5.4 %collective-permute-start.13 = (bf16[64,1024]{1,0:T(8,128)(2,1)S(1)}, bf16[64,1024]{1,0:T(8,128)(2,1)S(1)}, u32[]{:S(2)}, u32[]{:S(2)}) collective-permute-start(bf16[64,1024]{1,0:T(8,128)(2,1)S(1)} %broadcast_select_fusion.a0), channel_id=1, source_target_pairs={{0,2},{8,10},{32,34},{40,42},{64,66},{72,74},{96,98},{104,106},{12... | collective-permute-start | bytes 393224 | tf_op jit(solution)/shard_map/ppermute | solution.py:49
  38.3 1.5 %collective-permute-start.11 = (bf16[64,1024]{1,0:T(8,128)(2,1)S(1)}, bf16[64,1024]{1,0:T(8,128)(2,1)S(1)}, u32[]{:S(2)}, u32[]{:S(2)}) collective-permute-start(bf16[64,1024]{1,0:T(8,128)(2,1)S(1)} %broadcast_select_fusion.a0), channel_id=1, source_target_pairs={{0,1},{8,9},{32,33},{40,41},{64,65},{72,73},{96,97},{104,105},{128... | collective-permute-start | bytes 393224 | tf_op jit(solution)/shard_map/ppermute | solution.py:49
  39.8 2.0 %collective-permute-done.13.a3 = bf16[64,1024]{1,0:T(8,128)(2,1)S(1)} collective-permute-done((bf16[64,1024]{1,0:T(8,128)(2,1)S(1)}, bf16[64,1024]{1,0:T(8,128)(2,1)S(1)}, u32[]{:S(2)}, u32[]{:S(2)}) %collective-permute-start.13) | collective-permute-done | bytes 131104 | tf_op jit(solution)/shard_map/ppermute | solution.py:49
  42.5 1.2 %collective-permute-done.11.a1 = bf16[64,1024]{1,0:T(8,128)(2,1)S(1)} collective-permute-done((bf16[64,1024]{1,0:T(8,128)(2,1)S(1)}, bf16[64,1024]{1,0:T(8,128)(2,1)S(1)}, u32[]{:S(2)}, u32[]{:S(2)}) %collective-permute-start.11) | collective-permute-done | bytes 131104 | tf_op jit(solution)/shard_map/ppermute | solution.py:49
  43.7 2.8 %collective-permute-start.14 = (bf16[256,1024]{1,0:T(8,128)(2,1)S(1)}, bf16[256,1024]{1,0:T(8,128)(2,1)S(1)}, u32[]{:S(2)}, u32[]{:S(2)}) collective-permute-start(bf16[256,1024]{1,0:T(8,128)(2,1)S(1)} %pad_maximum_fusion), channel_id=1, source_target_pairs={{0,8},{8,0},{32,40},{40,32},{64,72},{72,64},{96,104},{104,96},{128... | collective-permute-start | bytes 1572872 | tf_op jit(solution)/shard_map/ppermute | solution.py:189
  46.6 1.5 %collective-permute-done.14.b_ref = bf16[256,1024]{1,0:T(8,128)(2,1)S(1)} collective-permute-done((bf16[256,1024]{1,0:T(8,128)(2,1)S(1)}, bf16[256,1024]{1,0:T(8,128)(2,1)S(1)}, u32[]{:S(2)}, u32[]{:S(2)}) %collective-permute-start.14) | collective-permute-done | bytes 524320 | tf_op jit(solution)/shard_map/ppermute | solution.py:189
  48.1 5.0 %anchor_attention.1 = bf16[64,4096]{1,0:T(8,128)(2,1)} custom-call(bf16[64,4096]{1,0:T(8,128)(2,1)S(1)} %copy-done, f32[8,256,128]{2,1,0:T(8,128)S(1)} %get-tuple-element.12.mix_ref, f32[8,256,128]{2,1,0:T(8,128)S(1)} %get-tuple-element.13.stat_ref, bf16[64,1024]{1,0:T(8,128)(2,1)S(1)} %broadcast_select_fusion.a0, ...), custom_call_target="tpu_custom_call" | custom-call | flops 268435456 | bytes 4194304 | tf_op jit(solution)/shard_map/anchor_attention/pallas_call | solution.py:165
  (18 shorter events, 2.3 us)
Async XLA Ops:
  1.0 5.4 %collective-permute-start = (bf16[64,1024]{1,0:T(8,128)(2,1)S(1)}, bf16[64,1024]{1,0:T(8,128)(2,1)S(1)}, u32[]{:S(2)}, u32[]{:S(2)}) collective-permute-start(bf16[64,1024]{1,0:T(8,128)(2,1)S(1)} %pad_maximum_fusion.2), channel_id=1, source_target_pairs={{0,8},{1,9},{2,10},{3,11}} | collective-permute-start | bytes 393224 | tf_op jit(solution)/shard_map/ppermute | solution.py:182
  6.4 4.3 %collective-permute-start.3 = (bf16[64,1024]{1,0:T(8,128)(2,1)S(1)}, bf16[64,1024]{1,0:T(8,128)(2,1)S(1)}, u32[]{:S(2)}, u32[]{:S(2)}) collective-permute-start(bf16[64,1024]{1,0:T(8,128)(2,1)S(1)} %maximum_select_fusion), channel_id=1, source_target_pairs={{0,16},{8,24},{1,17},{9,25},{2,18},{10,26},{3,19},{11,27}} | collective-permute-start | bytes 393224 | tf_op jit(solution)/shard_map/ppermute | solution.py:67
  7.7 4.3 %collective-permute-start.2 = (bf16[64,1024]{1,0:T(8,128)(2,1)S(1)}, bf16[64,1024]{1,0:T(8,128)(2,1)S(1)}, u32[]{:S(2)}, u32[]{:S(2)}) collective-permute-start(bf16[64,1024]{1,0:T(8,128)(2,1)S(1)} %maximum_select_fusion), channel_id=1, source_target_pairs={{0,20},{8,28},{1,21},{9,29},{2,22},{10,30},{3,23},{11,31}} | collective-permute-start | bytes 393224 | tf_op jit(solution)/shard_map/ppermute | solution.py:67
  9.0 4.7 %collective-permute-start.1 = (bf16[64,1024]{1,0:T(8,128)(2,1)S(1)}, bf16[64,1024]{1,0:T(8,128)(2,1)S(1)}, u32[]{:S(2)}, u32[]{:S(2)}) collective-permute-start(bf16[64,1024]{1,0:T(8,128)(2,1)S(1)} %maximum_select_fusion), channel_id=1, source_target_pairs={{0,4},{8,12},{1,5},{9,13},{2,6},{10,14},{3,7},{11,15}} | collective-permute-start | bytes 393224 | tf_op jit(solution)/shard_map/ppermute | solution.py:67
  13.7 18.0 %copy-start = (bf16[64,4096]{1,0:T(8,128)(2,1)S(1)}, bf16[64,4096]{1,0:T(8,128)(2,1)}, u32[]{:S(2)}) copy-start(bf16[64,4096]{1,0:T(8,128)(2,1)} %q_ref.3) | copy-start | bytes 1572868
  13.7 8.0 %collective-permute-start.6 = (bf16[64,1024]{1,0:T(8,128)(2,1)S(1)}, bf16[64,1024]{1,0:T(8,128)(2,1)S(1)}, u32[]{:S(2)}, u32[]{:S(2)}) collective-permute-start(bf16[64,1024]{1,0:T(8,128)(2,1)S(1)} %select_select_fusion.1), channel_id=1, source_target_pairs={{0,64},{8,72},{1,65},{9,73},{2,66},{10,74},{3,67},{11,75},{16,80},... | collective-permute-start | bytes 393224 | tf_op jit(solution)/shard_map/ppermute | solution.py:67
  15.1 9.1 %collective-permute-start.5 = (bf16[64,1024]{1,0:T(8,128)(2,1)S(1)}, bf16[64,1024]{1,0:T(8,128)(2,1)S(1)}, u32[]{:S(2)}, u32[]{:S(2)}) collective-permute-start(bf16[64,1024]{1,0:T(8,128)(2,1)S(1)} %select_select_fusion.1), channel_id=1, source_target_pairs={{0,192},{8,200},{1,193},{9,201},{2,194},{10,202},{3,195},{11,203},... | collective-permute-start | bytes 393224 | tf_op jit(solution)/shard_map/ppermute | solution.py:67
  16.4 7.8 %collective-permute-start.4 = (bf16[64,1024]{1,0:T(8,128)(2,1)S(1)}, bf16[64,1024]{1,0:T(8,128)(2,1)S(1)}, u32[]{:S(2)}, u32[]{:S(2)}) collective-permute-start(bf16[64,1024]{1,0:T(8,128)(2,1)S(1)} %select_select_fusion.1), channel_id=1, source_target_pairs={{0,128},{8,136},{1,129},{9,137},{2,130},{10,138},{3,131},{11,139},... | collective-permute-start | bytes 393224 | tf_op jit(solution)/shard_map/ppermute | solution.py:67
  17.8 12.6 %collective-permute-start.10 = (bf16[64,2048]{1,0:T(8,128)(2,1)S(1)}, bf16[64,2048]{1,0:T(8,128)(2,1)S(1)}, u32[]{:S(2)}, u32[]{:S(2)}) collective-permute-start(bf16[64,2048]{1,0:T(8,128)(2,1)S(1)} %pad_maximum_fusion.1.own_ref), channel_id=1, source_target_pairs={{0,3},{8,11},{32,35},{40,43},{64,67},{72,75},{96,99},{104,107},{12... | collective-permute-start | bytes 786440 | tf_op jit(solution)/shard_map/ppermute | solution.py:49
  20.4 10.0 %collective-permute-start.9 = (bf16[64,2048]{1,0:T(8,128)(2,1)S(1)}, bf16[64,2048]{1,0:T(8,128)(2,1)S(1)}, u32[]{:S(2)}, u32[]{:S(2)}) collective-permute-start(bf16[64,2048]{1,0:T(8,128)(2,1)S(1)} %pad_maximum_fusion.1.own_ref), channel_id=1, source_target_pairs={{0,2},{8,10},{32,34},{40,42},{64,66},{72,74},{96,98},{104,106},{12... | collective-permute-start | bytes 786440 | tf_op jit(solution)/shard_map/ppermute | solution.py:49
  21.7 9.9 %collective-permute-start.8 = (bf16[64,2048]{1,0:T(8,128)(2,1)S(1)}, bf16[64,2048]{1,0:T(8,128)(2,1)S(1)}, u32[]{:S(2)}, u32[]{:S(2)}) collective-permute-start(bf16[64,2048]{1,0:T(8,128)(2,1)S(1)} %pad_maximum_fusion.1.own_ref), channel_id=1, source_target_pairs={{0,1},{8,9},{32,33},{40,41},{64,65},{72,73},{96,97},{104,105},{128... | collective-permute-start | bytes 786440 | tf_op jit(solution)/shard_map/ppermute | solution.py:49
  24.3 8.5 %collective-permute-start.7 = (bf16[64,1024]{1,0:T(8,128)(2,1)S(1)}, bf16[64,1024]{1,0:T(8,128)(2,1)S(1)}, u32[]{:S(2)}, u32[]{:S(2)}) collective-permute-start(bf16[64,1024]{1,0:T(8,128)(2,1)S(1)} %select_select_fusion), channel_id=1, source_target_pairs={{0,32},{8,40},{1,33},{9,41},{2,34},{10,42},{3,35},{11,43},{16,48},... | collective-permute-start | bytes 393224 | tf_op jit(solution)/shard_map/ppermute | solution.py:67
  32.9 8.9 %collective-permute-start.13 = (bf16[64,1024]{1,0:T(8,128)(2,1)S(1)}, bf16[64,1024]{1,0:T(8,128)(2,1)S(1)}, u32[]{:S(2)}, u32[]{:S(2)}) collective-permute-start(bf16[64,1024]{1,0:T(8,128)(2,1)S(1)} %broadcast_select_fusion.a0), channel_id=1, source_target_pairs={{0,2},{8,10},{32,34},{40,42},{64,66},{72,74},{96,98},{104,106},{12... | collective-permute-start | bytes 393224 | tf_op jit(solution)/shard_map/ppermute | solution.py:49
  38.3 4.2 %collective-permute-start.12 = (bf16[64,1024]{1,0:T(8,128)(2,1)S(1)}, bf16[64,1024]{1,0:T(8,128)(2,1)S(1)}, u32[]{:S(2)}, u32[]{:S(2)}) collective-permute-start(bf16[64,1024]{1,0:T(8,128)(2,1)S(1)} %broadcast_select_fusion.a0), channel_id=1, source_target_pairs={{0,3},{8,11},{32,35},{40,43},{64,67},{72,75},{96,99},{104,107},{12... | collective-permute-start | bytes 393224 | tf_op jit(solution)/shard_map/ppermute | solution.py:49
  38.3 5.4 %collective-permute-start.11 = (bf16[64,1024]{1,0:T(8,128)(2,1)S(1)}, bf16[64,1024]{1,0:T(8,128)(2,1)S(1)}, u32[]{:S(2)}, u32[]{:S(2)}) collective-permute-start(bf16[64,1024]{1,0:T(8,128)(2,1)S(1)} %broadcast_select_fusion.a0), channel_id=1, source_target_pairs={{0,1},{8,9},{32,33},{40,41},{64,65},{72,73},{96,97},{104,105},{128... | collective-permute-start | bytes 393224 | tf_op jit(solution)/shard_map/ppermute | solution.py:49
  43.7 4.4 %collective-permute-start.14 = (bf16[256,1024]{1,0:T(8,128)(2,1)S(1)}, bf16[256,1024]{1,0:T(8,128)(2,1)S(1)}, u32[]{:S(2)}, u32[]{:S(2)}) collective-permute-start(bf16[256,1024]{1,0:T(8,128)(2,1)S(1)} %pad_maximum_fusion), channel_id=1, source_target_pairs={{0,8},{8,0},{32,40},{40,32},{64,72},{72,64},{96,104},{104,96},{128... | collective-permute-start | bytes 1572872 | tf_op jit(solution)/shard_map/ppermute | solution.py:189

commit v2 on v1

v2 whole, which is shorter than its diff:
```python
import functools

import jax
import jax.numpy as jnp
import numpy as np
from jax import lax
from jax.experimental import pallas as pl
from jax.experimental.pallas import tpu as pltpu
from jax.sharding import PartitionSpec as P

H = 32
KV = 8
HD = 128
BLK = 256
ROWS = 64
GROUP = H // KV
HALF = KV // 2
RATE = HD ** (-0.5) * 1.4426950408889634
AXES = ("blk", "hd")


def place(x, y, z, core):
    return (z * 4 + (x % 2) * 2 + core) * 8 + (x // 2) * 4 + y


def whereabouts():
    blk, hd = lax.axis_index("blk"), lax.axis_index("hd")
    return (hd >> 2) * 2 + ((blk >> 1) & 1), hd & 3, blk >> 2, blk & 1


def on_chips(chips):
    x, _, z, _ = whereabouts()
    bits = 0
    for a, b in chips:
        bits |= 1 << (a * 8 + b)
    shift = (x * 8 + z).astype(jnp.uint32)
    return ((jnp.uint32(np.uint32(bits)) >> shift) & 1) == 1


def chips():
    return [(x, y, z) for x in range(4) for y in range(4) for z in range(8)]


def along_y(array, step):
    pairs = [
        (place(x, y, z, core), place(x, (y + step) % 4, z, core))
        for x, y, z in chips()
        for core in range(2)
    ]
    return lax.ppermute(array, AXES, pairs)


def to_other_core(array):
    pairs = [(place(x, y, z, c), place(x, y, z, 1 - c)) for x, y, z in chips() for c in range(2)]
    return lax.ppermute(array, AXES, pairs)


def spread(piece, beside):
    have = [(0, 0)]
    for number, level in enumerate(LEVELS):
        came = []
        for step in level:
            moves = [((x, z), b) for x, z in have for b in step(x, z)]
            pairs = [
                (place(a[0], y, a[1], core), place(b[0], y, b[1], core))
                for a, b in moves
                for y in range(4)
                for core in range(2)
            ]
            came.append((lax.ppermute(piece, AXES, pairs), [b for _, b in moves]))
        if number == 2:
            got, beside = lax.optimization_barrier(([g for g, _ in came], beside))
            came = [(g, to) for g, (_, to) in zip(got, came)]
        for got, to in came:
            piece = jnp.where(on_chips(to), got, piece)
            have = have + to
    return piece, beside


def by(dx, dz):
    return lambda x, z: [((x + dx) % 4, (z + dz) % 8)]


LEVELS = (
    (by(1, 0), by(3, 0), by(2, 0)),
    (by(0, 2), by(0, 6), by(0, 4)),
    (by(0, 1),),
)


def stacked_queries(q_ref, start):
    return jnp.concatenate(
        [q_ref[:, pl.ds(start + i * HD, HD)] for i in range(GROUP)], axis=0
    )


def raw_scores(query, key):
    return lax.dot_general(query, key, (((1,), (1,)), ((), ())), preferred_element_type=jnp.float32)


def own_kernel(q_ref, own_ref, near_ref, far_ref, low_ref, high_ref, state_ref):
    y = lax.axis_index("hd") & 3
    rows = GROUP * ROWS
    row = lax.broadcasted_iota(jnp.int32, (rows, BLK), 0) & (ROWS - 1)
    column = lax.broadcasted_iota(jnp.int32, (rows, BLK), 1)
    behind = jnp.where(y >= 1, 2 * ROWS, 0)
    ahead = jnp.where(y == 3, 3 * ROWS, 0)
    across = jnp.where(y >= 2, 4 * ROWS, 0)
    end = jnp.where(
        column < ROWS,
        row + 1,
        jnp.where(column < 2 * ROWS, behind, jnp.where(column < 3 * ROWS, ahead, across)),
    )
    visible = column < end
    for g in range(KV):
        base = (g // HALF) * 2 * HALF * HD + (g % HALF) * HD
        far = low_ref if g < HALF else high_ref

        def part(base, offset):
            return jnp.concatenate(
                [r[:, base : base + HD] for r in (own_ref, near_ref, far_ref)]
                + [far[:, offset : offset + HD]],
                axis=0,
            )

        key = part(base, (g % HALF) * HD)
        value = part(base + HALF * HD, (HALF + g % HALF) * HD)
        masked = jnp.where(visible, raw_scores(stacked_queries(q_ref, g * GROUP * HD), key), -jnp.inf)
        largest = jnp.max(masked, axis=1, keepdims=True)
        raised = jnp.exp2((masked - largest) * RATE)
        totals = jnp.sum(raised, axis=1, keepdims=True)
        state_ref[g, :, :HD] = jnp.dot(
            raised.astype(jnp.bfloat16), value, preferred_element_type=jnp.float32
        )
        state_ref[g, :, HD : 2 * HD] = jnp.broadcast_to(largest, (rows, HD))
        state_ref[g, :, 2 * HD :] = jnp.broadcast_to(totals, (rows, HD))


def own_attention(queries, pieces):
    rows = GROUP * ROWS
    return pl.pallas_call(
        own_kernel,
        out_shape=jax.ShapeDtypeStruct((KV, rows, 3 * HD), jnp.float32),
        cost_estimate=pl.CostEstimate(
            flops=4 * KV * rows * BLK * HD, bytes_accessed=4 << 20, transcendentals=KV * rows * BLK
        ),
        compiler_params=pltpu.CompilerParams(vmem_limit_bytes=12 << 20),
        name="own_attention",
    )(queries, *pieces)


def anchor_kernel(last, q_ref, state_ref, *refs):
    blk, hd = lax.axis_index("blk"), lax.axis_index("hd")
    anchored = blk * 2 + (hd >> 2) > 0
    half = 1 - (blk & 1) if last else blk & 1
    width = HALF * GROUP * HD
    out_ref = refs[-1]
    pieces = refs[1:-1] if last else refs[:-1]
    for g in range(HALF):
        key = jnp.concatenate([r[:, g * HD : (g + 1) * HD] for r in pieces], axis=0)
        value = jnp.concatenate(
            [r[:, (HALF + g) * HD : (HALF + g + 1) * HD] for r in pieces], axis=0
        )
        head = half * HALF + g
        start = pl.multiple_of(head * GROUP * HD, GROUP * HD)
        scores = raw_scores(stacked_queries(q_ref, start), key)
        scores = jnp.where(anchored, scores, -jnp.inf)
        state = state_ref[head]
        old = state[:, HD : 2 * HD]
        largest = jnp.maximum(jnp.max(scores, axis=1, keepdims=True), old)
        raised = jnp.exp2((scores - jnp.concatenate([largest, largest], axis=1)) * RATE)
        keep = jnp.exp2((old - largest) * RATE)
        totals = jnp.sum(raised, axis=1, keepdims=True) + state[:, 2 * HD :] * keep
        mixture = jnp.dot(raised.astype(jnp.bfloat16), value, preferred_element_type=jnp.float32)
        result = ((mixture + state[:, :HD] * keep) / totals).astype(jnp.bfloat16)
        base = start if last else g * GROUP * HD
        for i in range(GROUP):
            out_ref[:, pl.ds(base + i * HD, HD)] = result[i * ROWS : (i + 1) * ROWS]
    if last:
        out_ref[:, pl.ds(pl.multiple_of((1 - half) * width, width), width)] = refs[0][...]


def anchor_attention(last, queries, own, *arrays):
    rows = GROUP * ROWS
    width = H * HD if last else H * HD // 2
    return pl.pallas_call(
        functools.partial(anchor_kernel, last),
        out_shape=jax.ShapeDtypeStruct((ROWS, width), jnp.bfloat16),
        cost_estimate=pl.CostEstimate(
            flops=4 * HALF * rows * BLK * HD,
            bytes_accessed=2 << 20,
            transcendentals=HALF * rows * BLK,
        ),
        compiler_params=pltpu.CompilerParams(vmem_limit_bytes=12 << 20),
        name="anchor_attention",
    )(queries, own, *arrays)


def shards(queries, keys, values):
    _, _, _, core = whereabouts()
    width = HALF * HD
    low = jnp.concatenate([keys[:, :width], values[:, :width]], axis=1)
    high = jnp.concatenate([keys[:, width:], values[:, width:]], axis=1)
    both = jnp.concatenate([low, high], axis=1)
    behind, ahead = along_y(both, 1), along_y(both, 3)
    pieces = [
        both,
        behind,
        ahead,
        along_y(behind[:, : 2 * width], 1),
        along_y(ahead[:, 2 * width :], 3),
    ]
    own = own_attention(queries, pieces)
    across = to_other_core(high)
    anchor, own = spread(jnp.where(core == 1, across, low), own)
    mine = [anchor] + [along_y(anchor, step) for step in (1, 3, 2)]
    other = to_other_core(jnp.concatenate(mine, axis=0))
    first = anchor_attention(False, queries, own, *mine)
    return anchor_attention(True, queries, own, first, other)


def solution(mesh):
    rows = P(("blk", "hd"), None)
    return jax.shard_map(
        shards, mesh=mesh, in_specs=(rows, rows, rows), out_specs=rows, check_vma=False
    )
```

time: 53.6 us -> 42.1 us (0.79)
  waiting for transfers between devices: 19 us -> 10.5 us
  Pallas kernels: 6.16 us -> 3.61 us
    ppermute x6 -> x7, starting transfers between devices: 13.3 us -> 7.28 us  [along_y(): return lax.ppermute(array, AXES, pairs)]
    ppermute x2, waiting for transfers between devices: 5.59 us -> 1.68 us  [to_other_core(): return lax.ppermute(array, AXES, pairs)]
    ppermute x7, waiting for transfers between devices: 3.35 us -> 0.02 us  [spread(): came.append((lax.ppermute(piece, AXES, pairs), [b for _, b in moves]))]
    ppermute x2, starting transfers between devices: 4.13 us -> 7.34 us  [to_other_core(): return lax.ppermute(array, AXES, pairs)]
    pallas_call x2 -> x3, Pallas kernels: 6.16 us -> 3.61 us  [the longest x2 2.48 us: anchor_attention(): pl.pallas_call(functools.partial(anchor_kernel, last), out_shape=jax.Shap...]
    ppermute x7, starting transfers between devices: 9.21 us -> 11.7 us  [spread(): came.append((lax.ppermute(piece, AXES, pairs), [b for _, b in moves]))]
    ppermute x6 -> x7, waiting for transfers between devices: 10 us -> 8.81 us  [along_y(): return lax.ppermute(array, AXES, pairs)]
  transfers between devices with their start and end apart: 15 -> 16, of which waited for: 10 -> 6; matrix products, arithmetic and copies ran while one was open for 0% -> 0% of each run, Pallas kernels for 2% -> 5%
where the time goes in v2:
time: 42.1 us; the launch traced here: 41.9 us
  starting transfers between devices  26.3 us (62%)
  waiting for transfers between devices  10.5 us (25%)
  Pallas kernels  3.61 us (9%)
  local copies, waits for them, and re-layouts  1.03 us (2%)
    ppermute x7, starting transfers between devices, spread(): came.append((lax.ppermute(piece, AXES, pairs), [b for _, b in moves]))  11.7 us
    ppermute x7, waiting for transfers between devices, along_y(): return lax.ppermute(array, AXES, pairs)  8.81 us
    ppermute x2, starting transfers between devices, to_other_core(): return lax.ppermute(array, AXES, pairs)  7.34 us
    ppermute x7, starting transfers between devices, along_y(): return lax.ppermute(array, AXES, pairs)  7.28 us
    pallas_call x2, Pallas kernels, anchor_attention(): pl.pallas_call(functools.partial(anchor_kernel, last), out_shape=jax.Shap...  2.48 us
    ppermute x2, waiting for transfers between devices, to_other_core(): return lax.ppermute(array, AXES, pairs)  1.68 us
    pallas_call x1, Pallas kernels, own_attention(): pl.pallas_call(own_kernel, out_shape=jax.ShapeDtypeStruct((KV, rows, 3 *...  1.13 us
    slice x1, local copies, waits for them, and re-layouts, shards(): low = jnp.concatenate([keys[:, :width], values[:, :width]], axis=1)  1.01 us
  transfers between devices with their start and end apart: 16, of which 6 were waited for; matrix products, arithmetic and copies ran while one was open for 0% of the time, Pallas kernels for 5%

profile of v2, /device:TPU:1, one launch (start us, length us, event | category | flops | bytes accessed | tf_op | source)
XLA Modules:
  0.0 41.9 jit_solution(473656366109822772)
XLA Ops:
  0.0 1.0 %fusion = (bf16[64,512]{1,0:T(8,128)(2,1)S(1)}, bf16[64,512]{1,0:T(8,128)(2,1)S(1)}, bf16[64,512]{1,0:T(8,128)(2,1)S(1)}, bf16[64,512]{1,0:T(8,128)(2,1)S(1)}) fusion(bf16[64,1024]{1,0:T(8,128)(2,1)} %param.4, bf16[64,1024]{1,0:T(8,128)(2,1)} %param.5), kind=kLoop, calls=%fused_computation.7 | loop fusion | bytes 524288 | tf_op jit(solution)/shard_map/slice | solution.py:202
  1.0 3.3 %collective-permute-start = (bf16[64,1024]{1,0:T(8,128)(2,1)S(1)}, bf16[64,1024]{1,0:T(8,128)(2,1)S(1)}, u32[]{:S(2)}, u32[]{:S(2)}) collective-permute-start(bf16[64,1024]{1,0:T(8,128)(2,1)S(1)} %pad_maximum_fusion.2), channel_id=1, source_target_pairs={{0,8},{8,0},{32,40},{40,32},{64,72},{72,64},{96,104},{104,96},{128... | collective-permute-start | bytes 393224 | tf_op jit(solution)/shard_map/ppermute | solution.py:55
  4.4 1.0 %collective-permute-done = bf16[64,1024]{1,0:T(8,128)(2,1)S(1)} collective-permute-done((bf16[64,1024]{1,0:T(8,128)(2,1)S(1)}, bf16[64,1024]{1,0:T(8,128)(2,1)S(1)}, u32[]{:S(2)}, u32[]{:S(2)}) %collective-permute-start) | collective-permute-done | bytes 131104 | tf_op jit(solution)/shard_map/ppermute | solution.py:55
  5.4 1.4 %collective-permute-start.3 = (bf16[64,1024]{1,0:T(8,128)(2,1)S(1)}, bf16[64,1024]{1,0:T(8,128)(2,1)S(1)}, u32[]{:S(2)}, u32[]{:S(2)}) collective-permute-start(bf16[64,1024]{1,0:T(8,128)(2,1)S(1)} %maximum_select_fusion), channel_id=1, source_target_pairs={{0,16},{8,24},{1,17},{9,25},{2,18},{10,26},{3,19},{11,27}} | collective-permute-start | bytes 393224 | tf_op jit(solution)/shard_map/ppermute | solution.py:70
  6.8 1.9 %collective-permute-start.2 = (bf16[64,1024]{1,0:T(8,128)(2,1)S(1)}, bf16[64,1024]{1,0:T(8,128)(2,1)S(1)}, u32[]{:S(2)}, u32[]{:S(2)}) collective-permute-start(bf16[64,1024]{1,0:T(8,128)(2,1)S(1)} %maximum_select_fusion), channel_id=1, source_target_pairs={{0,20},{8,28},{1,21},{9,29},{2,22},{10,30},{3,23},{11,31}} | collective-permute-start | bytes 393224 | tf_op jit(solution)/shard_map/ppermute | solution.py:70
  8.7 1.3 %collective-permute-start.1 = (bf16[64,1024]{1,0:T(8,128)(2,1)S(1)}, bf16[64,1024]{1,0:T(8,128)(2,1)S(1)}, u32[]{:S(2)}, u32[]{:S(2)}) collective-permute-start(bf16[64,1024]{1,0:T(8,128)(2,1)S(1)} %maximum_select_fusion), channel_id=1, source_target_pairs={{0,4},{8,12},{1,5},{9,13},{2,6},{10,14},{3,7},{11,15}} | collective-permute-start | bytes 393224 | tf_op jit(solution)/shard_map/ppermute | solution.py:70
  10.1 2.8 %collective-permute-start.9 = (bf16[64,2048]{1,0:T(8,128)(2,1)S(1)}, bf16[64,2048]{1,0:T(8,128)(2,1)S(1)}, u32[]{:S(2)}, u32[]{:S(2)}) collective-permute-start(bf16[64,2048]{1,0:T(8,128)(2,1)S(1)} %pad_maximum_fusion.1.own_ref), channel_id=1, source_target_pairs={{0,3},{8,11},{32,35},{40,43},{64,67},{72,75},{96,99},{104,107},{12... | collective-permute-start | bytes 786440 | tf_op jit(solution)/shard_map/ppermute | solution.py:50
  12.9 1.3 %collective-permute-start.6 = (bf16[64,1024]{1,0:T(8,128)(2,1)S(1)}, bf16[64,1024]{1,0:T(8,128)(2,1)S(1)}, u32[]{:S(2)}, u32[]{:S(2)}) collective-permute-start(bf16[64,1024]{1,0:T(8,128)(2,1)S(1)} %select_select_fusion.1), channel_id=1, source_target_pairs={{0,64},{8,72},{1,65},{9,73},{2,66},{10,74},{3,67},{11,75},{16,80},... | collective-permute-start | bytes 393224 | tf_op jit(solution)/shard_map/ppermute | solution.py:70
  14.2 3.0 %collective-permute-start.5 = (bf16[64,1024]{1,0:T(8,128)(2,1)S(1)}, bf16[64,1024]{1,0:T(8,128)(2,1)S(1)}, u32[]{:S(2)}, u32[]{:S(2)}) collective-permute-start(bf16[64,1024]{1,0:T(8,128)(2,1)S(1)} %select_select_fusion.1), channel_id=1, source_target_pairs={{0,192},{8,200},{1,193},{9,201},{2,194},{10,202},{3,195},{11,203},... | collective-permute-start | bytes 393224 | tf_op jit(solution)/shard_map/ppermute | solution.py:70
  17.2 1.6 %collective-permute-start.4 = (bf16[64,1024]{1,0:T(8,128)(2,1)S(1)}, bf16[64,1024]{1,0:T(8,128)(2,1)S(1)}, u32[]{:S(2)}, u32[]{:S(2)}) collective-permute-start(bf16[64,1024]{1,0:T(8,128)(2,1)S(1)} %select_select_fusion.1), channel_id=1, source_target_pairs={{0,128},{8,136},{1,129},{9,137},{2,130},{10,138},{3,131},{11,139},... | collective-permute-start | bytes 393224 | tf_op jit(solution)/shard_map/ppermute | solution.py:70
  18.8 2.7 %collective-permute-start.11 = (bf16[64,1024]{1,0:T(8,128)(2,1)S(1)}, bf16[64,1024]{1,0:T(8,128)(2,1)S(1)}, u32[]{:S(2)}, u32[]{:S(2)}) collective-permute-start(bf16[64,1024]{1,0:T(8,128)(2,1)S(1)} %slice.25), channel_id=1, source_target_pairs={{0,3},{8,11},{32,35},{40,43},{64,67},{72,75},{96,99},{104,107},{12... | collective-permute-start | bytes 393224 | tf_op jit(solution)/shard_map/ppermute | solution.py:50
  21.7 1.3 %collective-permute-start.7 = (bf16[64,1024]{1,0:T(8,128)(2,1)S(1)}, bf16[64,1024]{1,0:T(8,128)(2,1)S(1)}, u32[]{:S(2)}, u32[]{:S(2)}) collective-permute-start(bf16[64,1024]{1,0:T(8,128)(2,1)S(1)} %select_select_fusion), channel_id=1, source_target_pairs={{0,32},{8,40},{1,33},{9,41},{2,34},{10,42},{3,35},{11,43},{16,48},... | collective-permute-start | bytes 393224 | tf_op jit(solution)/shard_map/ppermute | solution.py:70
  23.0 0.5 %collective-permute-done.11.high_ref = bf16[64,1024]{1,0:T(8,128)(2,1)S(1)} collective-permute-done((bf16[64,1024]{1,0:T(8,128)(2,1)S(1)}, bf16[64,1024]{1,0:T(8,128)(2,1)S(1)}, u32[]{:S(2)}, u32[]{:S(2)}) %collective-permute-start.11) | collective-permute-done | bytes 131104 | tf_op jit(solution)/shard_map/ppermute | solution.py:50
  23.5 3.2 %collective-permute-done.10.low_ref = bf16[64,1024]{1,0:T(8,128)(2,1)S(1)} collective-permute-done((bf16[64,1024]{1,0:T(8,128)(2,1)S(1)}, bf16[64,1024]{1,0:T(8,128)(2,1)S(1)}, u32[]{:S(2)}, u32[]{:S(2)}) %collective-permute-start.10) | collective-permute-done | bytes 131104 | tf_op jit(solution)/shard_map/ppermute | solution.py:50
  26.7 1.1 %own_attention.1.state_ref = f32[8,256,384]{2,1,0:T(8,128)S(1)} custom-call(bf16[64,4096]{1,0:T(8,128)(2,1)S(1)} %copy-done, bf16[64,2048]{1,0:T(8,128)(2,1)S(1)} %pad_maximum_fusion.1.own_ref, bf16[64,2048]{1,0:T(8,128)(2,1)S(1)} %collective-permute-done.8.near_ref, bf16[64,2048]{1,0:T(8,128)(2,1)S(1)} %collective-permute-done.9.far_ref, ...), custom_call_target="tpu_custom_call" | custom-call | flops 268435456 | bytes 4194304 | tf_op jit(solution)/shard_map/own_attention/pallas_call | solution.py:141
  27.8 0.1 collective-permute-start.14
  27.9 1.2 %collective-permute-start.13 = (bf16[64,1024]{1,0:T(8,128)(2,1)S(1)}, bf16[64,1024]{1,0:T(8,128)(2,1)S(1)}, u32[]{:S(2)}, u32[]{:S(2)}) collective-permute-start(bf16[64,1024]{1,0:T(8,128)(2,1)S(1)} %broadcast_select_fusion.refs_0_), channel_id=1, source_target_pairs={{0,3},{8,11},{32,35},{40,43},{64,67},{72,75},{96,99},{104,107},{12... | collective-permute-start | bytes 393224 | tf_op jit(solution)/shard_map/ppermute | solution.py:50
  29.1 0.4 collective-permute-start.12
  29.5 3.8 %collective-permute-done.14.refs_3_ = bf16[64,1024]{1,0:T(8,128)(2,1)S(1)} collective-permute-done((bf16[64,1024]{1,0:T(8,128)(2,1)S(1)}, bf16[64,1024]{1,0:T(8,128)(2,1)S(1)}, u32[]{:S(2)}, u32[]{:S(2)}) %collective-permute-start.14) | collective-permute-done | bytes 131104 | tf_op jit(solution)/shard_map/ppermute | solution.py:50
  33.3 1.3 %collective-permute-done.12.refs_1_ = bf16[64,1024]{1,0:T(8,128)(2,1)S(1)} collective-permute-done((bf16[64,1024]{1,0:T(8,128)(2,1)S(1)}, bf16[64,1024]{1,0:T(8,128)(2,1)S(1)}, u32[]{:S(2)}, u32[]{:S(2)}) %collective-permute-start.12) | collective-permute-done | bytes 131104 | tf_op jit(solution)/shard_map/ppermute | solution.py:50
  34.7 4.0 %collective-permute-start.15 = (bf16[256,1024]{1,0:T(8,128)(2,1)S(1)}, bf16[256,1024]{1,0:T(8,128)(2,1)S(1)}, u32[]{:S(2)}, u32[]{:S(2)}) collective-permute-start(bf16[256,1024]{1,0:T(8,128)(2,1)S(1)} %pad_maximum_fusion), channel_id=1, source_target_pairs={{0,8},{8,0},{32,40},{40,32},{64,72},{72,64},{96,104},{104,96},{128... | collective-permute-start | bytes 1572872 | tf_op jit(solution)/shard_map/ppermute | solution.py:55
  38.7 0.8 %anchor_attention.2.refs_0_ = bf16[64,2048]{1,0:T(8,128)(2,1)S(1)} custom-call(bf16[64,4096]{1,0:T(8,128)(2,1)S(1)} %copy-done, f32[8,256,384]{2,1,0:T(8,128)S(1)} %own_attention.1.state_ref, bf16[64,1024]{1,0:T(8,128)(2,1)S(1)} %broadcast_select_fusion.refs_0_, bf16[64,1024]{1,0:T(8,128)(2,1)S(1)} %collective-permute-done.12.refs_1_, ...), custom_call_target="tpu_custom_call" | custom-call | flops 134217728 | bytes 2097152 | tf_op jit(solution)/shard_map/anchor_attention/pallas_call | solution.py:186
  39.6 0.7 %collective-permute-done.15.refs_1_ = bf16[256,1024]{1,0:T(8,128)(2,1)S(1)} collective-permute-done((bf16[256,1024]{1,0:T(8,128)(2,1)S(1)}, bf16[256,1024]{1,0:T(8,128)(2,1)S(1)}, u32[]{:S(2)}, u32[]{:S(2)}) %collective-permute-start.15) | collective-permute-done | bytes 524320 | tf_op jit(solution)/shard_map/ppermute | solution.py:55
  40.2 1.6 %anchor_attention.3 = bf16[64,4096]{1,0:T(8,128)(2,1)} custom-call(bf16[64,4096]{1,0:T(8,128)(2,1)S(1)} %copy-done, f32[8,256,384]{2,1,0:T(8,128)S(1)} %own_attention.1.state_ref, bf16[64,2048]{1,0:T(8,128)(2,1)S(1)} %anchor_attention.2.refs_0_, bf16[256,1024]{1,0:T(8,128)(2,1)S(1)} %collective-permute-done.15.refs_1_), custom_call_target="tpu_custom_call" | custom-call | flops 134217728 | bytes 2097152 | tf_op jit(solution)/shard_map/anchor_attention/pallas_call | solution.py:186
  (23 shorter events, 0.3 us)
Async XLA Ops:
  0.0 26.7 %copy-start = (bf16[64,4096]{1,0:T(8,128)(2,1)S(1)}, bf16[64,4096]{1,0:T(8,128)(2,1)}, u32[]{:S(2)}) copy-start(bf16[64,4096]{1,0:T(8,128)(2,1)} %q_ref.5) | copy-start | bytes 1572868
  1.0 4.3 %collective-permute-start = (bf16[64,1024]{1,0:T(8,128)(2,1)S(1)}, bf16[64,1024]{1,0:T(8,128)(2,1)S(1)}, u32[]{:S(2)}, u32[]{:S(2)}) collective-permute-start(bf16[64,1024]{1,0:T(8,128)(2,1)S(1)} %pad_maximum_fusion.2), channel_id=1, source_target_pairs={{0,8},{8,0},{32,40},{40,32},{64,72},{72,64},{96,104},{104,96},{128... | collective-permute-start | bytes 393224 | tf_op jit(solution)/shard_map/ppermute | solution.py:55
  5.4 7.5 %collective-permute-start.3 = (bf16[64,1024]{1,0:T(8,128)(2,1)S(1)}, bf16[64,1024]{1,0:T(8,128)(2,1)S(1)}, u32[]{:S(2)}, u32[]{:S(2)}) collective-permute-start(bf16[64,1024]{1,0:T(8,128)(2,1)S(1)} %maximum_select_fusion), channel_id=1, source_target_pairs={{0,16},{8,24},{1,17},{9,25},{2,18},{10,26},{3,19},{11,27}} | collective-permute-start | bytes 393224 | tf_op jit(solution)/shard_map/ppermute | solution.py:70
  6.8 6.1 %collective-permute-start.2 = (bf16[64,1024]{1,0:T(8,128)(2,1)S(1)}, bf16[64,1024]{1,0:T(8,128)(2,1)S(1)}, u32[]{:S(2)}, u32[]{:S(2)}) collective-permute-start(bf16[64,1024]{1,0:T(8,128)(2,1)S(1)} %maximum_select_fusion), channel_id=1, source_target_pairs={{0,20},{8,28},{1,21},{9,29},{2,22},{10,30},{3,23},{11,31}} | collective-permute-start | bytes 393224 | tf_op jit(solution)/shard_map/ppermute | solution.py:70
  8.7 4.2 %collective-permute-start.1 = (bf16[64,1024]{1,0:T(8,128)(2,1)S(1)}, bf16[64,1024]{1,0:T(8,128)(2,1)S(1)}, u32[]{:S(2)}, u32[]{:S(2)}) collective-permute-start(bf16[64,1024]{1,0:T(8,128)(2,1)S(1)} %maximum_select_fusion), channel_id=1, source_target_pairs={{0,4},{8,12},{1,5},{9,13},{2,6},{10,14},{3,7},{11,15}} | collective-permute-start | bytes 393224 | tf_op jit(solution)/shard_map/ppermute | solution.py:70
  10.1 8.7 %collective-permute-start.9 = (bf16[64,2048]{1,0:T(8,128)(2,1)S(1)}, bf16[64,2048]{1,0:T(8,128)(2,1)S(1)}, u32[]{:S(2)}, u32[]{:S(2)}) collective-permute-start(bf16[64,2048]{1,0:T(8,128)(2,1)S(1)} %pad_maximum_fusion.1.own_ref), channel_id=1, source_target_pairs={{0,3},{8,11},{32,35},{40,43},{64,67},{72,75},{96,99},{104,107},{12... | collective-permute-start | bytes 786440 | tf_op jit(solution)/shard_map/ppermute | solution.py:50
  12.9 8.7 %collective-permute-start.8 = (bf16[64,2048]{1,0:T(8,128)(2,1)S(1)}, bf16[64,2048]{1,0:T(8,128)(2,1)S(1)}, u32[]{:S(2)}, u32[]{:S(2)}) collective-permute-start(bf16[64,2048]{1,0:T(8,128)(2,1)S(1)} %pad_maximum_fusion.1.own_ref), channel_id=1, source_target_pairs={{0,1},{8,9},{32,33},{40,41},{64,65},{72,73},{96,97},{104,105},{128... | collective-permute-start | bytes 786440 | tf_op jit(solution)/shard_map/ppermute | solution.py:50
  12.9 8.7 %collective-permute-start.6 = (bf16[64,1024]{1,0:T(8,128)(2,1)S(1)}, bf16[64,1024]{1,0:T(8,128)(2,1)S(1)}, u32[]{:S(2)}, u32[]{:S(2)}) collective-permute-start(bf16[64,1024]{1,0:T(8,128)(2,1)S(1)} %select_select_fusion.1), channel_id=1, source_target_pairs={{0,64},{8,72},{1,65},{9,73},{2,66},{10,74},{3,67},{11,75},{16,80},... | collective-permute-start | bytes 393224 | tf_op jit(solution)/shard_map/ppermute | solution.py:70
  14.2 7.4 %collective-permute-start.5 = (bf16[64,1024]{1,0:T(8,128)(2,1)S(1)}, bf16[64,1024]{1,0:T(8,128)(2,1)S(1)}, u32[]{:S(2)}, u32[]{:S(2)}) collective-permute-start(bf16[64,1024]{1,0:T(8,128)(2,1)S(1)} %select_select_fusion.1), channel_id=1, source_target_pairs={{0,192},{8,200},{1,193},{9,201},{2,194},{10,202},{3,195},{11,203},... | collective-permute-start | bytes 393224 | tf_op jit(solution)/shard_map/ppermute | solution.py:70
  17.2 4.5 %collective-permute-start.4 = (bf16[64,1024]{1,0:T(8,128)(2,1)S(1)}, bf16[64,1024]{1,0:T(8,128)(2,1)S(1)}, u32[]{:S(2)}, u32[]{:S(2)}) collective-permute-start(bf16[64,1024]{1,0:T(8,128)(2,1)S(1)} %select_select_fusion.1), channel_id=1, source_target_pairs={{0,128},{8,136},{1,129},{9,137},{2,130},{10,138},{3,131},{11,139},... | collective-permute-start | bytes 393224 | tf_op jit(solution)/shard_map/ppermute | solution.py:70
  18.8 4.7 %collective-permute-start.11 = (bf16[64,1024]{1,0:T(8,128)(2,1)S(1)}, bf16[64,1024]{1,0:T(8,128)(2,1)S(1)}, u32[]{:S(2)}, u32[]{:S(2)}) collective-permute-start(bf16[64,1024]{1,0:T(8,128)(2,1)S(1)} %slice.25), channel_id=1, source_target_pairs={{0,3},{8,11},{32,35},{40,43},{64,67},{72,75},{96,99},{104,107},{12... | collective-permute-start | bytes 393224 | tf_op jit(solution)/shard_map/ppermute | solution.py:50
  21.6 5.1 %collective-permute-start.10 = (bf16[64,1024]{1,0:T(8,128)(2,1)S(1)}, bf16[64,1024]{1,0:T(8,128)(2,1)S(1)}, u32[]{:S(2)}, u32[]{:S(2)}) collective-permute-start(bf16[64,1024]{1,0:T(8,128)(2,1)S(1)} %slice.24), channel_id=1, source_target_pairs={{0,1},{8,9},{32,33},{40,41},{64,65},{72,73},{96,97},{104,105},{128... | collective-permute-start | bytes 393224 | tf_op jit(solution)/shard_map/ppermute | solution.py:50
  21.7 6.1 %collective-permute-start.7 = (bf16[64,1024]{1,0:T(8,128)(2,1)S(1)}, bf16[64,1024]{1,0:T(8,128)(2,1)S(1)}, u32[]{:S(2)}, u32[]{:S(2)}) collective-permute-start(bf16[64,1024]{1,0:T(8,128)(2,1)S(1)} %select_select_fusion), channel_id=1, source_target_pairs={{0,32},{8,40},{1,33},{9,41},{2,34},{10,42},{3,35},{11,43},{16,48},... | collective-permute-start | bytes 393224 | tf_op jit(solution)/shard_map/ppermute | solution.py:70
  27.8 5.5 %collective-permute-start.14 = (bf16[64,1024]{1,0:T(8,128)(2,1)S(1)}, bf16[64,1024]{1,0:T(8,128)(2,1)S(1)}, u32[]{:S(2)}, u32[]{:S(2)}) collective-permute-start(bf16[64,1024]{1,0:T(8,128)(2,1)S(1)} %broadcast_select_fusion.refs_0_), channel_id=1, source_target_pairs={{0,2},{8,10},{32,34},{40,42},{64,66},{72,74},{96,98},{104,106},{12... | collective-permute-start | bytes 393224 | tf_op jit(solution)/shard_map/ppermute | solution.py:50
  27.9 5.4 %collective-permute-start.13 = (bf16[64,1024]{1,0:T(8,128)(2,1)S(1)}, bf16[64,1024]{1,0:T(8,128)(2,1)S(1)}, u32[]{:S(2)}, u32[]{:S(2)}) collective-permute-start(bf16[64,1024]{1,0:T(8,128)(2,1)S(1)} %broadcast_select_fusion.refs_0_), channel_id=1, source_target_pairs={{0,3},{8,11},{32,35},{40,43},{64,67},{72,75},{96,99},{104,107},{12... | collective-permute-start | bytes 393224 | tf_op jit(solution)/shard_map/ppermute | solution.py:50
  29.1 5.5 %collective-permute-start.12 = (bf16[64,1024]{1,0:T(8,128)(2,1)S(1)}, bf16[64,1024]{1,0:T(8,128)(2,1)S(1)}, u32[]{:S(2)}, u32[]{:S(2)}) collective-permute-start(bf16[64,1024]{1,0:T(8,128)(2,1)S(1)} %broadcast_select_fusion.refs_0_), channel_id=1, source_target_pairs={{0,1},{8,9},{32,33},{40,41},{64,65},{72,73},{96,97},{104,105},{128... | collective-permute-start | bytes 393224 | tf_op jit(solution)/shard_map/ppermute | solution.py:50
  34.7 5.6 %collective-permute-start.15 = (bf16[256,1024]{1,0:T(8,128)(2,1)S(1)}, bf16[256,1024]{1,0:T(8,128)(2,1)S(1)}, u32[]{:S(2)}, u32[]{:S(2)}) collective-permute-start(bf16[256,1024]{1,0:T(8,128)(2,1)S(1)} %pad_maximum_fusion), channel_id=1, source_target_pairs={{0,8},{8,0},{32,40},{40,32},{64,72},{72,64},{96,104},{104,96},{128... | collective-permute-start | bytes 1572872 | tf_op jit(solution)/shard_map/ppermute | solution.py:55

commit v3 on v2

--- a/solution.py
+++ b/solution.py
@@ -68,7 +68,7 @@
                 for core in range(2)
             ]
             came.append((lax.ppermute(piece, AXES, pairs), [b for _, b in moves]))
-        if number == 2:
+        if number == 1:
             got, beside = lax.optimization_barrier(([g for g, _ in came], beside))
             came = [(g, to) for g, (_, to) in zip(got, came)]
         for got, to in came:
@@ -83,8 +83,8 @@
 
 LEVELS = (
     (by(1, 0), by(3, 0), by(2, 0)),
-    (by(0, 2), by(0, 6), by(0, 4)),
-    (by(0, 1),),
+    (by(0, 2), by(0, 6)),
+    (lambda x, z: {2: [(x, 4)], 6: [(x, 5)]}.get(z, []), lambda x, z: [(x, {0: 1, 2: 3, 6: 7}[z])]),
 )
 
 
@@ -203,18 +203,13 @@
     high = jnp.concatenate([keys[:, width:], values[:, width:]], axis=1)
     both = jnp.concatenate([low, high], axis=1)
     behind, ahead = along_y(both, 1), along_y(both, 3)
-    pieces = [
-        both,
-        behind,
-        ahead,
-        along_y(behind[:, : 2 * width], 1),
-        along_y(ahead[:, 2 * width :], 3),
-    ]
-    own = own_attention(queries, pieces)
     across = to_other_core(high)
-    anchor, own = spread(jnp.where(core == 1, across, low), own)
-    mine = [anchor] + [along_y(anchor, step) for step in (1, 3, 2)]
-    other = to_other_core(jnp.concatenate(mine, axis=0))
+    anchor, (behind, ahead) = spread(jnp.where(core == 1, across, low), (behind, ahead))
+    far = along_y(behind[:, : 2 * width], 1), along_y(ahead[:, 2 * width :], 3)
+    own = own_attention(queries, [both, behind, ahead, *far])
+    mine = [anchor] + [along_y(anchor, step) for step in (2, 1, 3)]
+    joined, own = lax.optimization_barrier((jnp.concatenate(mine, axis=0), own))
+    other = to_other_core(joined)
     first = anchor_attention(False, queries, own, *mine)
     return anchor_attention(True, queries, own, first, other)
 

time: 42.1 us -> 38.9 us (0.924)
  waiting for transfers between devices: 10.5 us -> 7.59 us
    ppermute x7, waiting for transfers between devices: 8.81 us -> 5.9 us  [along_y(): return lax.ppermute(array, AXES, pairs)]
    ppermute x7, starting transfers between devices: 7.28 us -> 9.57 us  [along_y(): return lax.ppermute(array, AXES, pairs)]
    ppermute x2, starting transfers between devices: 7.34 us -> 5.66 us  [to_other_core(): return lax.ppermute(array, AXES, pairs)]
    ppermute x7, starting transfers between devices: 11.7 us -> 10.8 us  [spread(): came.append((lax.ppermute(piece, AXES, pairs), [b for _, b in moves]))]
where the time goes in v3:
time: 38.9 us; the launch traced here: 38.6 us
  starting transfers between devices  26.1 us (67%)
  waiting for transfers between devices  7.59 us (20%)
  Pallas kernels  3.61 us (9%)
  local copies, waits for them, and re-layouts  1.03 us (3%)
    ppermute x7, starting transfers between devices, spread(): came.append((lax.ppermute(piece, AXES, pairs), [b for _, b in moves]))  10.8 us
    ppermute x7, starting transfers between devices, along_y(): return lax.ppermute(array, AXES, pairs)  9.57 us
    ppermute x7, waiting for transfers between devices, along_y(): return lax.ppermute(array, AXES, pairs)  5.9 us
    ppermute x2, starting transfers between devices, to_other_core(): return lax.ppermute(array, AXES, pairs)  5.66 us
    pallas_call x2, Pallas kernels, anchor_attention(): pl.pallas_call(functools.partial(anchor_kernel, last), out_shape=jax.Shap...  2.48 us
    ppermute x2, waiting for transfers between devices, to_other_core(): return lax.ppermute(array, AXES, pairs)  1.68 us
    pallas_call x1, Pallas kernels, own_attention(): pl.pallas_call(own_kernel, out_shape=jax.ShapeDtypeStruct((KV, rows, 3 *...  1.13 us
    slice x1, local copies, waits for them, and re-layouts, shards(): low = jnp.concatenate([keys[:, :width], values[:, :width]], axis=1)  1.01 us
  transfers between devices with their start and end apart: 16, of which 6 were waited for; matrix products, arithmetic and copies ran while one was open for 0% of the time, Pallas kernels for 5%

profile of v3, /device:TPU:1, one launch (start us, length us, event | category | flops | bytes accessed | tf_op | source)
XLA Modules:
  0.0 38.6 jit_solution(17577032027509939403)
XLA Ops:
  0.0 1.0 %fusion = (bf16[64,512]{1,0:T(8,128)(2,1)S(1)}, bf16[64,512]{1,0:T(8,128)(2,1)S(1)}, bf16[64,512]{1,0:T(8,128)(2,1)S(1)}, bf16[64,512]{1,0:T(8,128)(2,1)S(1)}) fusion(bf16[64,1024]{1,0:T(8,128)(2,1)} %param.4, bf16[64,1024]{1,0:T(8,128)(2,1)} %param.5), kind=kLoop, calls=%fused_computation.7 | loop fusion | bytes 524288 | tf_op jit(solution)/shard_map/slice | solution.py:202
  1.0 3.3 %collective-permute-start = (bf16[64,1024]{1,0:T(8,128)(2,1)S(1)}, bf16[64,1024]{1,0:T(8,128)(2,1)S(1)}, u32[]{:S(2)}, u32[]{:S(2)}) collective-permute-start(bf16[64,1024]{1,0:T(8,128)(2,1)S(1)} %pad_maximum_fusion.2), channel_id=1, source_target_pairs={{0,8},{8,0},{32,40},{40,32},{64,72},{72,64},{96,104},{104,96},{128... | collective-permute-start | bytes 393224 | tf_op jit(solution)/shard_map/ppermute | solution.py:55
  4.4 1.0 %collective-permute-done = bf16[64,1024]{1,0:T(8,128)(2,1)S(1)} collective-permute-done((bf16[64,1024]{1,0:T(8,128)(2,1)S(1)}, bf16[64,1024]{1,0:T(8,128)(2,1)S(1)}, u32[]{:S(2)}, u32[]{:S(2)}) %collective-permute-start) | collective-permute-done | bytes 131104 | tf_op jit(solution)/shard_map/ppermute | solution.py:55
  5.4 2.9 %collective-permute-start.1 = (bf16[64,1024]{1,0:T(8,128)(2,1)S(1)}, bf16[64,1024]{1,0:T(8,128)(2,1)S(1)}, u32[]{:S(2)}, u32[]{:S(2)}) collective-permute-start(bf16[64,1024]{1,0:T(8,128)(2,1)S(1)} %maximum_select_fusion), channel_id=1, source_target_pairs={{0,4},{8,12},{1,5},{9,13},{2,6},{10,14},{3,7},{11,15}} | collective-permute-start | bytes 393224 | tf_op jit(solution)/shard_map/ppermute | solution.py:70
  8.3 1.3 %collective-permute-start.2 = (bf16[64,1024]{1,0:T(8,128)(2,1)S(1)}, bf16[64,1024]{1,0:T(8,128)(2,1)S(1)}, u32[]{:S(2)}, u32[]{:S(2)}) collective-permute-start(bf16[64,1024]{1,0:T(8,128)(2,1)S(1)} %maximum_select_fusion), channel_id=1, source_target_pairs={{0,20},{8,28},{1,21},{9,29},{2,22},{10,30},{3,23},{11,31}} | collective-permute-start | bytes 393224 | tf_op jit(solution)/shard_map/ppermute | solution.py:70
  9.6 1.3 %collective-permute-start.3 = (bf16[64,1024]{1,0:T(8,128)(2,1)S(1)}, bf16[64,1024]{1,0:T(8,128)(2,1)S(1)}, u32[]{:S(2)}, u32[]{:S(2)}) collective-permute-start(bf16[64,1024]{1,0:T(8,128)(2,1)S(1)} %maximum_select_fusion), channel_id=1, source_target_pairs={{0,16},{8,24},{1,17},{9,25},{2,18},{10,26},{3,19},{11,27}} | collective-permute-start | bytes 393224 | tf_op jit(solution)/shard_map/ppermute | solution.py:70
  11.0 1.4 %collective-permute-start.6 = (bf16[64,2048]{1,0:T(8,128)(2,1)S(1)}, bf16[64,2048]{1,0:T(8,128)(2,1)S(1)}, u32[]{:S(2)}, u32[]{:S(2)}) collective-permute-start(bf16[64,2048]{1,0:T(8,128)(2,1)S(1)} %pad_maximum_fusion.1.own_ref), channel_id=1, source_target_pairs={{0,1},{8,9},{32,33},{40,41},{64,65},{72,73},{96,97},{104,105},{128... | collective-permute-start | bytes 786440 | tf_op jit(solution)/shard_map/ppermute | solution.py:50
  12.3 1.5 %collective-permute-start.7 = (bf16[64,2048]{1,0:T(8,128)(2,1)S(1)}, bf16[64,2048]{1,0:T(8,128)(2,1)S(1)}, u32[]{:S(2)}, u32[]{:S(2)}) collective-permute-start(bf16[64,2048]{1,0:T(8,128)(2,1)S(1)} %pad_maximum_fusion.1.own_ref), channel_id=1, source_target_pairs={{0,3},{8,11},{32,35},{40,43},{64,67},{72,75},{96,99},{104,107},{12... | collective-permute-start | bytes 786440 | tf_op jit(solution)/shard_map/ppermute | solution.py:50
  13.9 1.3 %collective-permute-start.4 = (bf16[64,1024]{1,0:T(8,128)(2,1)S(1)}, bf16[64,1024]{1,0:T(8,128)(2,1)S(1)}, u32[]{:S(2)}, u32[]{:S(2)}) collective-permute-start(bf16[64,1024]{1,0:T(8,128)(2,1)S(1)} %select_select_fusion.2), channel_id=1, source_target_pairs={{0,64},{8,72},{1,65},{9,73},{2,66},{10,74},{3,67},{11,75},{16,80},... | collective-permute-start | bytes 393224 | tf_op jit(solution)/shard_map/ppermute | solution.py:70
  15.2 2.1 %collective-permute-start.5 = (bf16[64,1024]{1,0:T(8,128)(2,1)S(1)}, bf16[64,1024]{1,0:T(8,128)(2,1)S(1)}, u32[]{:S(2)}, u32[]{:S(2)}) collective-permute-start(bf16[64,1024]{1,0:T(8,128)(2,1)S(1)} %select_select_fusion.2), channel_id=1, source_target_pairs={{0,192},{8,200},{1,193},{9,201},{2,194},{10,202},{3,195},{11,203},... | collective-permute-start | bytes 393224 | tf_op jit(solution)/shard_map/ppermute | solution.py:70
  17.3 2.3 %collective-permute-done.6.near_ref = bf16[64,2048]{1,0:T(8,128)(2,1)S(1)} collective-permute-done((bf16[64,2048]{1,0:T(8,128)(2,1)S(1)}, bf16[64,2048]{1,0:T(8,128)(2,1)S(1)}, u32[]{:S(2)}, u32[]{:S(2)}) %collective-permute-start.6) | collective-permute-done | bytes 262176 | tf_op jit(solution)/shard_map/ppermute | solution.py:50
  19.6 1.3 %collective-permute-start.8 = (bf16[64,1024]{1,0:T(8,128)(2,1)S(1)}, bf16[64,1024]{1,0:T(8,128)(2,1)S(1)}, u32[]{:S(2)}, u32[]{:S(2)}) collective-permute-start(bf16[64,1024]{1,0:T(8,128)(2,1)S(1)} %select_select_fusion.1), channel_id=1, source_target_pairs={{0,32},{8,40},{1,33},{9,41},{2,34},{10,42},{3,35},{11,43},{16,48},... | collective-permute-start | bytes 393224 | tf_op jit(solution)/shard_map/ppermute | solution.py:70
  21.6 1.0 %collective-permute-start.13 = (bf16[64,1024]{1,0:T(8,128)(2,1)S(1)}, bf16[64,1024]{1,0:T(8,128)(2,1)S(1)}, u32[]{:S(2)}, u32[]{:S(2)}) collective-permute-start(bf16[64,1024]{1,0:T(8,128)(2,1)S(1)} %slice.22), channel_id=1, source_target_pairs={{0,1},{8,9},{32,33},{40,41},{64,65},{72,73},{96,97},{104,105},{128... | collective-permute-start | bytes 393224 | tf_op jit(solution)/shard_map/ppermute | solution.py:50
  22.6 1.8 %collective-permute-start.14 = (bf16[64,1024]{1,0:T(8,128)(2,1)S(1)}, bf16[64,1024]{1,0:T(8,128)(2,1)S(1)}, u32[]{:S(2)}, u32[]{:S(2)}) collective-permute-start(bf16[64,1024]{1,0:T(8,128)(2,1)S(1)} %slice.23), channel_id=1, source_target_pairs={{0,3},{8,11},{32,35},{40,43},{64,67},{72,75},{96,99},{104,107},{12... | collective-permute-start | bytes 393224 | tf_op jit(solution)/shard_map/ppermute | solution.py:50
  24.5 1.2 %collective-permute-start.10 = (bf16[64,1024]{1,0:T(8,128)(2,1)S(1)}, bf16[64,1024]{1,0:T(8,128)(2,1)S(1)}, u32[]{:S(2)}, u32[]{:S(2)}) collective-permute-start(bf16[64,1024]{1,0:T(8,128)(2,1)S(1)} %select_select_fusion.refs_0_), channel_id=1, source_target_pairs={{0,2},{8,10},{32,34},{40,42},{64,66},{72,74},{96,98},{104,106},{12... | collective-permute-start | bytes 393224 | tf_op jit(solution)/shard_map/ppermute | solution.py:50
  25.7 0.8 %collective-permute-start.11 = (bf16[64,1024]{1,0:T(8,128)(2,1)S(1)}, bf16[64,1024]{1,0:T(8,128)(2,1)S(1)}, u32[]{:S(2)}, u32[]{:S(2)}) collective-permute-start(bf16[64,1024]{1,0:T(8,128)(2,1)S(1)} %select_select_fusion.refs_0_), channel_id=1, source_target_pairs={{0,1},{8,9},{32,33},{40,41},{64,65},{72,73},{96,97},{104,105},{128... | collective-permute-start | bytes 393224 | tf_op jit(solution)/shard_map/ppermute | solution.py:50
  26.5 1.9 %collective-permute-start.12 = (bf16[64,1024]{1,0:T(8,128)(2,1)S(1)}, bf16[64,1024]{1,0:T(8,128)(2,1)S(1)}, u32[]{:S(2)}, u32[]{:S(2)}) collective-permute-start(bf16[64,1024]{1,0:T(8,128)(2,1)S(1)} %select_select_fusion.refs_0_), channel_id=1, source_target_pairs={{0,3},{8,11},{32,35},{40,43},{64,67},{72,75},{96,99},{104,107},{12... | collective-permute-start | bytes 393224 | tf_op jit(solution)/shard_map/ppermute | solution.py:50
  28.4 1.1 %own_attention.1.state_ref = f32[8,256,384]{2,1,0:T(8,128)S(1)} custom-call(bf16[64,4096]{1,0:T(8,128)(2,1)S(1)} %copy-done, bf16[64,2048]{1,0:T(8,128)(2,1)S(1)} %pad_maximum_fusion.1.own_ref, bf16[64,2048]{1,0:T(8,128)(2,1)S(1)} %collective-permute-done.6.near_ref, bf16[64,2048]{1,0:T(8,128)(2,1)S(1)} %collective-permute-done.7.far_ref, ...), custom_call_target="tpu_custom_call" | custom-call | flops 268435456 | bytes 4194304 | tf_op jit(solution)/shard_map/own_attention/pallas_call | solution.py:141
  29.5 2.1 %collective-permute-done.10.refs_1_ = bf16[64,1024]{1,0:T(8,128)(2,1)S(1)} collective-permute-done((bf16[64,1024]{1,0:T(8,128)(2,1)S(1)}, bf16[64,1024]{1,0:T(8,128)(2,1)S(1)}, u32[]{:S(2)}, u32[]{:S(2)}) %collective-permute-start.10) | collective-permute-done | bytes 131104 | tf_op jit(solution)/shard_map/ppermute | solution.py:50
  31.6 0.8 %collective-permute-done.11.refs_2_ = bf16[64,1024]{1,0:T(8,128)(2,1)S(1)} collective-permute-done((bf16[64,1024]{1,0:T(8,128)(2,1)S(1)}, bf16[64,1024]{1,0:T(8,128)(2,1)S(1)}, u32[]{:S(2)}, u32[]{:S(2)}) %collective-permute-start.11) | collective-permute-done | bytes 131104 | tf_op jit(solution)/shard_map/ppermute | solution.py:50
  33.1 2.3 %collective-permute-start.15 = (bf16[256,1024]{1,0:T(8,128)(2,1)S(1)}, bf16[256,1024]{1,0:T(8,128)(2,1)S(1)}, u32[]{:S(2)}, u32[]{:S(2)}) collective-permute-start(bf16[256,1024]{1,0:T(8,128)(2,1)S(1)} %pad_maximum_fusion), channel_id=1, source_target_pairs={{0,8},{8,0},{32,40},{40,32},{64,72},{72,64},{96,104},{104,96},{128... | collective-permute-start | bytes 1572872 | tf_op jit(solution)/shard_map/ppermute | solution.py:55
  35.5 0.8 %anchor_attention.2.refs_0_ = bf16[64,2048]{1,0:T(8,128)(2,1)S(1)} custom-call(bf16[64,4096]{1,0:T(8,128)(2,1)S(1)} %copy-done, f32[8,256,384]{2,1,0:T(8,128)S(1)} %own_attention.1.state_ref, bf16[64,1024]{1,0:T(8,128)(2,1)S(1)} %select_select_fusion.refs_0_, bf16[64,1024]{1,0:T(8,128)(2,1)S(1)} %collective-permute-done.10.refs_1_, ...), custom_call_target="tpu_custom_call" | custom-call | flops 134217728 | bytes 2097152 | tf_op jit(solution)/shard_map/anchor_attention/pallas_call | solution.py:186
  36.3 0.7 %collective-permute-done.15.refs_1_ = bf16[256,1024]{1,0:T(8,128)(2,1)S(1)} collective-permute-done((bf16[256,1024]{1,0:T(8,128)(2,1)S(1)}, bf16[256,1024]{1,0:T(8,128)(2,1)S(1)}, u32[]{:S(2)}, u32[]{:S(2)}) %collective-permute-start.15) | collective-permute-done | bytes 524320 | tf_op jit(solution)/shard_map/ppermute | solution.py:55
  37.0 1.6 %anchor_attention.3 = bf16[64,4096]{1,0:T(8,128)(2,1)} custom-call(bf16[64,4096]{1,0:T(8,128)(2,1)S(1)} %copy-done, f32[8,256,384]{2,1,0:T(8,128)S(1)} %own_attention.1.state_ref, bf16[64,2048]{1,0:T(8,128)(2,1)S(1)} %anchor_attention.2.refs_0_, bf16[256,1024]{1,0:T(8,128)(2,1)S(1)} %collective-permute-done.15.refs_1_), custom_call_target="tpu_custom_call" | custom-call | flops 134217728 | bytes 2097152 | tf_op jit(solution)/shard_map/anchor_attention/pallas_call | solution.py:186
  (23 shorter events, 1.5 us)
Async XLA Ops:
  0.0 28.4 %copy-start = (bf16[64,4096]{1,0:T(8,128)(2,1)S(1)}, bf16[64,4096]{1,0:T(8,128)(2,1)}, u32[]{:S(2)}) copy-start(bf16[64,4096]{1,0:T(8,128)(2,1)} %q_ref.5) | copy-start | bytes 1572868
  1.0 4.3 %collective-permute-start = (bf16[64,1024]{1,0:T(8,128)(2,1)S(1)}, bf16[64,1024]{1,0:T(8,128)(2,1)S(1)}, u32[]{:S(2)}, u32[]{:S(2)}) collective-permute-start(bf16[64,1024]{1,0:T(8,128)(2,1)S(1)} %pad_maximum_fusion.2), channel_id=1, source_target_pairs={{0,8},{8,0},{32,40},{40,32},{64,72},{72,64},{96,104},{104,96},{128... | collective-permute-start | bytes 393224 | tf_op jit(solution)/shard_map/ppermute | solution.py:55
  5.4 8.5 %collective-permute-start.1 = (bf16[64,1024]{1,0:T(8,128)(2,1)S(1)}, bf16[64,1024]{1,0:T(8,128)(2,1)S(1)}, u32[]{:S(2)}, u32[]{:S(2)}) collective-permute-start(bf16[64,1024]{1,0:T(8,128)(2,1)S(1)} %maximum_select_fusion), channel_id=1, source_target_pairs={{0,4},{8,12},{1,5},{9,13},{2,6},{10,14},{3,7},{11,15}} | collective-permute-start | bytes 393224 | tf_op jit(solution)/shard_map/ppermute | solution.py:70
  8.3 5.5 %collective-permute-start.2 = (bf16[64,1024]{1,0:T(8,128)(2,1)S(1)}, bf16[64,1024]{1,0:T(8,128)(2,1)S(1)}, u32[]{:S(2)}, u32[]{:S(2)}) collective-permute-start(bf16[64,1024]{1,0:T(8,128)(2,1)S(1)} %maximum_select_fusion), channel_id=1, source_target_pairs={{0,20},{8,28},{1,21},{9,29},{2,22},{10,30},{3,23},{11,31}} | collective-permute-start | bytes 393224 | tf_op jit(solution)/shard_map/ppermute | solution.py:70
  9.6 4.2 %collective-permute-start.3 = (bf16[64,1024]{1,0:T(8,128)(2,1)S(1)}, bf16[64,1024]{1,0:T(8,128)(2,1)S(1)}, u32[]{:S(2)}, u32[]{:S(2)}) collective-permute-start(bf16[64,1024]{1,0:T(8,128)(2,1)S(1)} %maximum_select_fusion), channel_id=1, source_target_pairs={{0,16},{8,24},{1,17},{9,25},{2,18},{10,26},{3,19},{11,27}} | collective-permute-start | bytes 393224 | tf_op jit(solution)/shard_map/ppermute | solution.py:70
  11.0 8.6 %collective-permute-start.6 = (bf16[64,2048]{1,0:T(8,128)(2,1)S(1)}, bf16[64,2048]{1,0:T(8,128)(2,1)S(1)}, u32[]{:S(2)}, u32[]{:S(2)}) collective-permute-start(bf16[64,2048]{1,0:T(8,128)(2,1)S(1)} %pad_maximum_fusion.1.own_ref), channel_id=1, source_target_pairs={{0,1},{8,9},{32,33},{40,41},{64,65},{72,73},{96,97},{104,105},{128... | collective-permute-start | bytes 786440 | tf_op jit(solution)/shard_map/ppermute | solution.py:50
  12.3 7.3 %collective-permute-start.7 = (bf16[64,2048]{1,0:T(8,128)(2,1)S(1)}, bf16[64,2048]{1,0:T(8,128)(2,1)S(1)}, u32[]{:S(2)}, u32[]{:S(2)}) collective-permute-start(bf16[64,2048]{1,0:T(8,128)(2,1)S(1)} %pad_maximum_fusion.1.own_ref), channel_id=1, source_target_pairs={{0,3},{8,11},{32,35},{40,43},{64,67},{72,75},{96,99},{104,107},{12... | collective-permute-start | bytes 786440 | tf_op jit(solution)/shard_map/ppermute | solution.py:50
  13.9 5.7 %collective-permute-start.4 = (bf16[64,1024]{1,0:T(8,128)(2,1)S(1)}, bf16[64,1024]{1,0:T(8,128)(2,1)S(1)}, u32[]{:S(2)}, u32[]{:S(2)}) collective-permute-start(bf16[64,1024]{1,0:T(8,128)(2,1)S(1)} %select_select_fusion.2), channel_id=1, source_target_pairs={{0,64},{8,72},{1,65},{9,73},{2,66},{10,74},{3,67},{11,75},{16,80},... | collective-permute-start | bytes 393224 | tf_op jit(solution)/shard_map/ppermute | solution.py:70
  15.2 4.4 %collective-permute-start.5 = (bf16[64,1024]{1,0:T(8,128)(2,1)S(1)}, bf16[64,1024]{1,0:T(8,128)(2,1)S(1)}, u32[]{:S(2)}, u32[]{:S(2)}) collective-permute-start(bf16[64,1024]{1,0:T(8,128)(2,1)S(1)} %select_select_fusion.2), channel_id=1, source_target_pairs={{0,192},{8,200},{1,193},{9,201},{2,194},{10,202},{3,195},{11,203},... | collective-permute-start | bytes 393224 | tf_op jit(solution)/shard_map/ppermute | solution.py:70
  19.6 4.9 %collective-permute-start.8 = (bf16[64,1024]{1,0:T(8,128)(2,1)S(1)}, bf16[64,1024]{1,0:T(8,128)(2,1)S(1)}, u32[]{:S(2)}, u32[]{:S(2)}) collective-permute-start(bf16[64,1024]{1,0:T(8,128)(2,1)S(1)} %select_select_fusion.1), channel_id=1, source_target_pairs={{0,32},{8,40},{1,33},{9,41},{2,34},{10,42},{3,35},{11,43},{16,48},... | collective-permute-start | bytes 393224 | tf_op jit(solution)/shard_map/ppermute | solution.py:70
  20.9 3.6 %collective-permute-start.9 = (bf16[64,1024]{1,0:T(8,128)(2,1)S(1)}, bf16[64,1024]{1,0:T(8,128)(2,1)S(1)}, u32[]{:S(2)}, u32[]{:S(2)}) collective-permute-start(bf16[64,1024]{1,0:T(8,128)(2,1)S(1)} %select_select_fusion.1), channel_id=1, source_target_pairs={{64,128},{72,136},{65,129},{73,137},{66,130},{74,138},{67,131},{75... | collective-permute-start | bytes 393224 | tf_op jit(solution)/shard_map/ppermute | solution.py:70
  21.6 6.7 %collective-permute-start.13 = (bf16[64,1024]{1,0:T(8,128)(2,1)S(1)}, bf16[64,1024]{1,0:T(8,128)(2,1)S(1)}, u32[]{:S(2)}, u32[]{:S(2)}) collective-permute-start(bf16[64,1024]{1,0:T(8,128)(2,1)S(1)} %slice.22), channel_id=1, source_target_pairs={{0,1},{8,9},{32,33},{40,41},{64,65},{72,73},{96,97},{104,105},{128... | collective-permute-start | bytes 393224 | tf_op jit(solution)/shard_map/ppermute | solution.py:50
  22.6 5.7 %collective-permute-start.14 = (bf16[64,1024]{1,0:T(8,128)(2,1)S(1)}, bf16[64,1024]{1,0:T(8,128)(2,1)S(1)}, u32[]{:S(2)}, u32[]{:S(2)}) collective-permute-start(bf16[64,1024]{1,0:T(8,128)(2,1)S(1)} %slice.23), channel_id=1, source_target_pairs={{0,3},{8,11},{32,35},{40,43},{64,67},{72,75},{96,99},{104,107},{12... | collective-permute-start | bytes 393224 | tf_op jit(solution)/shard_map/ppermute | solution.py:50
  24.5 7.1 %collective-permute-start.10 = (bf16[64,1024]{1,0:T(8,128)(2,1)S(1)}, bf16[64,1024]{1,0:T(8,128)(2,1)S(1)}, u32[]{:S(2)}, u32[]{:S(2)}) collective-permute-start(bf16[64,1024]{1,0:T(8,128)(2,1)S(1)} %select_select_fusion.refs_0_), channel_id=1, source_target_pairs={{0,2},{8,10},{32,34},{40,42},{64,66},{72,74},{96,98},{104,106},{12... | collective-permute-start | bytes 393224 | tf_op jit(solution)/shard_map/ppermute | solution.py:50
  25.7 6.8 %collective-permute-start.11 = (bf16[64,1024]{1,0:T(8,128)(2,1)S(1)}, bf16[64,1024]{1,0:T(8,128)(2,1)S(1)}, u32[]{:S(2)}, u32[]{:S(2)}) collective-permute-start(bf16[64,1024]{1,0:T(8,128)(2,1)S(1)} %select_select_fusion.refs_0_), channel_id=1, source_target_pairs={{0,1},{8,9},{32,33},{40,41},{64,65},{72,73},{96,97},{104,105},{128... | collective-permute-start | bytes 393224 | tf_op jit(solution)/shard_map/ppermute | solution.py:50
  26.5 6.6 %collective-permute-start.12 = (bf16[64,1024]{1,0:T(8,128)(2,1)S(1)}, bf16[64,1024]{1,0:T(8,128)(2,1)S(1)}, u32[]{:S(2)}, u32[]{:S(2)}) collective-permute-start(bf16[64,1024]{1,0:T(8,128)(2,1)S(1)} %select_select_fusion.refs_0_), channel_id=1, source_target_pairs={{0,3},{8,11},{32,35},{40,43},{64,67},{72,75},{96,99},{104,107},{12... | collective-permute-start | bytes 393224 | tf_op jit(solution)/shard_map/ppermute | solution.py:50
  33.1 3.9 %collective-permute-start.15 = (bf16[256,1024]{1,0:T(8,128)(2,1)S(1)}, bf16[256,1024]{1,0:T(8,128)(2,1)S(1)}, u32[]{:S(2)}, u32[]{:S(2)}) collective-permute-start(bf16[256,1024]{1,0:T(8,128)(2,1)S(1)} %pad_maximum_fusion), channel_id=1, source_target_pairs={{0,8},{8,0},{32,40},{40,32},{64,72},{72,64},{96,104},{104,96},{128... | collective-permute-start | bytes 1572872 | tf_op jit(solution)/shard_map/ppermute | solution.py:55

commit v4 on v3

--- a/solution.py
+++ b/solution.py
@@ -83,8 +83,11 @@
 
 LEVELS = (
     (by(1, 0), by(3, 0), by(2, 0)),
-    (by(0, 2), by(0, 6)),
-    (lambda x, z: {2: [(x, 4)], 6: [(x, 5)]}.get(z, []), lambda x, z: [(x, {0: 1, 2: 3, 6: 7}[z])]),
+    (by(0, 3), by(0, 6)),
+    (
+        lambda x, z: [(x, {3: 4, 6: 5}[z])] if z else [],
+        lambda x, z: [(x, {0: 1, 3: 2, 6: 7}[z])],
+    ),
 )
 
 
@@ -203,7 +206,7 @@
     high = jnp.concatenate([keys[:, width:], values[:, width:]], axis=1)
     both = jnp.concatenate([low, high], axis=1)
     behind, ahead = along_y(both, 1), along_y(both, 3)
-    across = to_other_core(high)
+    across = lax.ppermute(high, AXES, [(place(0, y, 0, 0), place(0, y, 0, 1)) for y in range(4)])
     anchor, (behind, ahead) = spread(jnp.where(core == 1, across, low), (behind, ahead))
     far = along_y(behind[:, : 2 * width], 1), along_y(ahead[:, 2 * width :], 3)
     own = own_attention(queries, [both, behind, ahead, *far])

time: 38.9 us -> 38.1 us (0.979)
  starting transfers between devices: 26.1 us -> 21.3 us
  waiting for transfers between devices: 7.59 us -> 11.7 us
    ppermute x0 -> x1, waiting for transfers between devices: none -> 4.05 us  [shards(): lax.ppermute(high, AXES, [(place(0, y, 0, 0), place(0, y, 0, 1)) for y in...]
    ppermute x2 -> x1, starting transfers between devices: 5.66 us -> 2.11 us  [to_other_core(): return lax.ppermute(array, AXES, pairs)]
    ppermute x7, starting transfers between devices: 10.8 us -> 8.62 us  [spread(): came.append((lax.ppermute(piece, AXES, pairs), [b for _, b in moves]))]
    ppermute x0 -> x1, starting transfers between devices: none -> 1.29 us  [shards(): lax.ppermute(high, AXES, [(place(0, y, 0, 0), place(0, y, 0, 1)) for y in...]
    ppermute x2 -> x1, waiting for transfers between devices: 1.68 us -> 0.69 us  [to_other_core(): return lax.ppermute(array, AXES, pairs)]
    ppermute x7, waiting for transfers between devices: 5.9 us -> 6.61 us  [along_y(): return lax.ppermute(array, AXES, pairs)]
  transfers between devices with their start and end apart: 16 -> 16, of which waited for: 6 -> 7; matrix products, arithmetic and copies ran while one was open for 0% -> 0% of each run, Pallas kernels for 5% -> 5%
where the time goes in v4:
time: 38.1 us; the launch traced here: 37.9 us
  starting transfers between devices  21.3 us (56%)
  waiting for transfers between devices  11.7 us (31%)
  Pallas kernels  3.61 us (9%)
  local copies, waits for them, and re-layouts  1.03 us (3%)
    ppermute x7, starting transfers between devices, along_y(): return lax.ppermute(array, AXES, pairs)  9.24 us
    ppermute x7, starting transfers between devices, spread(): came.append((lax.ppermute(piece, AXES, pairs), [b for _, b in moves]))  8.62 us
    ppermute x7, waiting for transfers between devices, along_y(): return lax.ppermute(array, AXES, pairs)  6.61 us
    ppermute x1, waiting for transfers between devices, shards(): lax.ppermute(high, AXES, [(place(0, y, 0, 0), place(0, y, 0, 1)) for y in...  4.05 us
    pallas_call x2, Pallas kernels, anchor_attention(): pl.pallas_call(functools.partial(anchor_kernel, last), out_shape=jax.Shap...  2.48 us
    ppermute x1, starting transfers between devices, to_other_core(): return lax.ppermute(array, AXES, pairs)  2.11 us
    ppermute x1, starting transfers between devices, shards(): lax.ppermute(high, AXES, [(place(0, y, 0, 0), place(0, y, 0, 1)) for y in...  1.29 us
    pallas_call x1, Pallas kernels, own_attention(): pl.pallas_call(own_kernel, out_shape=jax.ShapeDtypeStruct((KV, rows, 3 *...  1.13 us
  transfers between devices with their start and end apart: 16, of which 7 were waited for; matrix products, arithmetic and copies ran while one was open for 0% of the time, Pallas kernels for 5%

profile of v4, /device:TPU:1, one launch (start us, length us, event | category | flops | bytes accessed | tf_op | source)
XLA Modules:
  0.0 37.9 jit_solution(9986661301560312296)
XLA Ops:
  0.0 1.0 %fusion = (bf16[64,512]{1,0:T(8,128)(2,1)S(1)}, bf16[64,512]{1,0:T(8,128)(2,1)S(1)}, bf16[64,512]{1,0:T(8,128)(2,1)S(1)}, bf16[64,512]{1,0:T(8,128)(2,1)S(1)}) fusion(bf16[64,1024]{1,0:T(8,128)(2,1)} %param.4, bf16[64,1024]{1,0:T(8,128)(2,1)} %param.5), kind=kLoop, calls=%fused_computation.7 | loop fusion | bytes 524288 | tf_op jit(solution)/shard_map/slice | solution.py:205
  1.0 1.3 %collective-permute-start = (bf16[64,1024]{1,0:T(8,128)(2,1)S(1)}, bf16[64,1024]{1,0:T(8,128)(2,1)S(1)}, u32[]{:S(2)}, u32[]{:S(2)}) collective-permute-start(bf16[64,1024]{1,0:T(8,128)(2,1)S(1)} %pad_maximum_fusion.2), channel_id=1, source_target_pairs={{0,8},{1,9},{2,10},{3,11}} | collective-permute-start | bytes 393224 | tf_op jit(solution)/shard_map/ppermute | solution.py:209
  2.3 4.1 %collective-permute-done = bf16[64,1024]{1,0:T(8,128)(2,1)S(1)} collective-permute-done((bf16[64,1024]{1,0:T(8,128)(2,1)S(1)}, bf16[64,1024]{1,0:T(8,128)(2,1)S(1)}, u32[]{:S(2)}, u32[]{:S(2)}) %collective-permute-start) | collective-permute-done | bytes 131104 | tf_op jit(solution)/shard_map/ppermute | solution.py:209
  6.4 1.3 %collective-permute-start.1 = (bf16[64,1024]{1,0:T(8,128)(2,1)S(1)}, bf16[64,1024]{1,0:T(8,128)(2,1)S(1)}, u32[]{:S(2)}, u32[]{:S(2)}) collective-permute-start(bf16[64,1024]{1,0:T(8,128)(2,1)S(1)} %maximum_select_fusion), channel_id=1, source_target_pairs={{0,4},{8,12},{1,5},{9,13},{2,6},{10,14},{3,7},{11,15}} | collective-permute-start | bytes 393224 | tf_op jit(solution)/shard_map/ppermute | solution.py:70
  7.7 1.3 %collective-permute-start.2 = (bf16[64,1024]{1,0:T(8,128)(2,1)S(1)}, bf16[64,1024]{1,0:T(8,128)(2,1)S(1)}, u32[]{:S(2)}, u32[]{:S(2)}) collective-permute-start(bf16[64,1024]{1,0:T(8,128)(2,1)S(1)} %maximum_select_fusion), channel_id=1, source_target_pairs={{0,20},{8,28},{1,21},{9,29},{2,22},{10,30},{3,23},{11,31}} | collective-permute-start | bytes 393224 | tf_op jit(solution)/shard_map/ppermute | solution.py:70
  9.0 1.3 %collective-permute-start.3 = (bf16[64,1024]{1,0:T(8,128)(2,1)S(1)}, bf16[64,1024]{1,0:T(8,128)(2,1)S(1)}, u32[]{:S(2)}, u32[]{:S(2)}) collective-permute-start(bf16[64,1024]{1,0:T(8,128)(2,1)S(1)} %maximum_select_fusion), channel_id=1, source_target_pairs={{0,16},{8,24},{1,17},{9,25},{2,18},{10,26},{3,19},{11,27}} | collective-permute-start | bytes 393224 | tf_op jit(solution)/shard_map/ppermute | solution.py:70
  10.4 0.9 %collective-permute-start.6 = (bf16[64,2048]{1,0:T(8,128)(2,1)S(1)}, bf16[64,2048]{1,0:T(8,128)(2,1)S(1)}, u32[]{:S(2)}, u32[]{:S(2)}) collective-permute-start(bf16[64,2048]{1,0:T(8,128)(2,1)S(1)} %pad_maximum_fusion.1.own_ref), channel_id=1, source_target_pairs={{0,1},{8,9},{32,33},{40,41},{64,65},{72,73},{96,97},{104,105},{128... | collective-permute-start | bytes 786440 | tf_op jit(solution)/shard_map/ppermute | solution.py:50
  11.3 1.9 %collective-permute-start.7 = (bf16[64,2048]{1,0:T(8,128)(2,1)S(1)}, bf16[64,2048]{1,0:T(8,128)(2,1)S(1)}, u32[]{:S(2)}, u32[]{:S(2)}) collective-permute-start(bf16[64,2048]{1,0:T(8,128)(2,1)S(1)} %pad_maximum_fusion.1.own_ref), channel_id=1, source_target_pairs={{0,3},{8,11},{32,35},{40,43},{64,67},{72,75},{96,99},{104,107},{12... | collective-permute-start | bytes 786440 | tf_op jit(solution)/shard_map/ppermute | solution.py:50
  13.4 1.3 %collective-permute-start.4 = (bf16[64,1024]{1,0:T(8,128)(2,1)S(1)}, bf16[64,1024]{1,0:T(8,128)(2,1)S(1)}, u32[]{:S(2)}, u32[]{:S(2)}) collective-permute-start(bf16[64,1024]{1,0:T(8,128)(2,1)S(1)} %select_select_fusion.2), channel_id=1, source_target_pairs={{0,96},{8,104},{1,97},{9,105},{2,98},{10,106},{3,99},{11,107},{16,... | collective-permute-start | bytes 393224 | tf_op jit(solution)/shard_map/ppermute | solution.py:70
  14.8 1.5 %collective-permute-start.5 = (bf16[64,1024]{1,0:T(8,128)(2,1)S(1)}, bf16[64,1024]{1,0:T(8,128)(2,1)S(1)}, u32[]{:S(2)}, u32[]{:S(2)}) collective-permute-start(bf16[64,1024]{1,0:T(8,128)(2,1)S(1)} %select_select_fusion.2), channel_id=1, source_target_pairs={{0,192},{8,200},{1,193},{9,201},{2,194},{10,202},{3,195},{11,203},... | collective-permute-start | bytes 393224 | tf_op jit(solution)/shard_map/ppermute | solution.py:70
  16.2 2.8 %collective-permute-done.6.near_ref = bf16[64,2048]{1,0:T(8,128)(2,1)S(1)} collective-permute-done((bf16[64,2048]{1,0:T(8,128)(2,1)S(1)}, bf16[64,2048]{1,0:T(8,128)(2,1)S(1)}, u32[]{:S(2)}, u32[]{:S(2)}) %collective-permute-start.6) | collective-permute-done | bytes 262176 | tf_op jit(solution)/shard_map/ppermute | solution.py:50
  19.1 1.3 %collective-permute-start.8 = (bf16[64,1024]{1,0:T(8,128)(2,1)S(1)}, bf16[64,1024]{1,0:T(8,128)(2,1)S(1)}, u32[]{:S(2)}, u32[]{:S(2)}) collective-permute-start(bf16[64,1024]{1,0:T(8,128)(2,1)S(1)} %select_select_fusion.1), channel_id=1, source_target_pairs={{0,32},{8,40},{1,33},{9,41},{2,34},{10,42},{3,35},{11,43},{16,48},... | collective-permute-start | bytes 393224 | tf_op jit(solution)/shard_map/ppermute | solution.py:70
  20.4 0.7 %collective-permute-start.9 = (bf16[64,1024]{1,0:T(8,128)(2,1)S(1)}, bf16[64,1024]{1,0:T(8,128)(2,1)S(1)}, u32[]{:S(2)}, u32[]{:S(2)}) collective-permute-start(bf16[64,1024]{1,0:T(8,128)(2,1)S(1)} %select_select_fusion.1), channel_id=1, source_target_pairs={{96,128},{104,136},{97,129},{105,137},{98,130},{106,138},{99,131},... | collective-permute-start | bytes 393224 | tf_op jit(solution)/shard_map/ppermute | solution.py:70
  21.3 2.7 %collective-permute-start.14 = (bf16[64,1024]{1,0:T(8,128)(2,1)S(1)}, bf16[64,1024]{1,0:T(8,128)(2,1)S(1)}, u32[]{:S(2)}, u32[]{:S(2)}) collective-permute-start(bf16[64,1024]{1,0:T(8,128)(2,1)S(1)} %slice.23), channel_id=1, source_target_pairs={{0,3},{8,11},{32,35},{40,43},{64,67},{72,75},{96,99},{104,107},{12... | collective-permute-start | bytes 393224 | tf_op jit(solution)/shard_map/ppermute | solution.py:50
  24.0 1.0 %collective-permute-start.10 = (bf16[64,1024]{1,0:T(8,128)(2,1)S(1)}, bf16[64,1024]{1,0:T(8,128)(2,1)S(1)}, u32[]{:S(2)}, u32[]{:S(2)}) collective-permute-start(bf16[64,1024]{1,0:T(8,128)(2,1)S(1)} %select_select_fusion.refs_0_), channel_id=1, source_target_pairs={{0,2},{8,10},{32,34},{40,42},{64,66},{72,74},{96,98},{104,106},{12... | collective-permute-start | bytes 393224 | tf_op jit(solution)/shard_map/ppermute | solution.py:50
  25.0 0.8 %collective-permute-start.11 = (bf16[64,1024]{1,0:T(8,128)(2,1)S(1)}, bf16[64,1024]{1,0:T(8,128)(2,1)S(1)}, u32[]{:S(2)}, u32[]{:S(2)}) collective-permute-start(bf16[64,1024]{1,0:T(8,128)(2,1)S(1)} %select_select_fusion.refs_0_), channel_id=1, source_target_pairs={{0,1},{8,9},{32,33},{40,41},{64,65},{72,73},{96,97},{104,105},{128... | collective-permute-start | bytes 393224 | tf_op jit(solution)/shard_map/ppermute | solution.py:50
  25.8 1.9 %collective-permute-start.12 = (bf16[64,1024]{1,0:T(8,128)(2,1)S(1)}, bf16[64,1024]{1,0:T(8,128)(2,1)S(1)}, u32[]{:S(2)}, u32[]{:S(2)}) collective-permute-start(bf16[64,1024]{1,0:T(8,128)(2,1)S(1)} %select_select_fusion.refs_0_), channel_id=1, source_target_pairs={{0,3},{8,11},{32,35},{40,43},{64,67},{72,75},{96,99},{104,107},{12... | collective-permute-start | bytes 393224 | tf_op jit(solution)/shard_map/ppermute | solution.py:50
  27.6 1.1 %own_attention.1.state_ref = f32[8,256,384]{2,1,0:T(8,128)S(1)} custom-call(bf16[64,4096]{1,0:T(8,128)(2,1)S(1)} %copy-done, bf16[64,2048]{1,0:T(8,128)(2,1)S(1)} %pad_maximum_fusion.1.own_ref, bf16[64,2048]{1,0:T(8,128)(2,1)S(1)} %collective-permute-done.6.near_ref, bf16[64,2048]{1,0:T(8,128)(2,1)S(1)} %collective-permute-done.7.far_ref, ...), custom_call_target="tpu_custom_call" | custom-call | flops 268435456 | bytes 4194304 | tf_op jit(solution)/shard_map/own_attention/pallas_call | solution.py:144
  28.8 2.3 %collective-permute-done.10.refs_1_ = bf16[64,1024]{1,0:T(8,128)(2,1)S(1)} collective-permute-done((bf16[64,1024]{1,0:T(8,128)(2,1)S(1)}, bf16[64,1024]{1,0:T(8,128)(2,1)S(1)}, u32[]{:S(2)}, u32[]{:S(2)}) %collective-permute-start.10) | collective-permute-done | bytes 131104 | tf_op jit(solution)/shard_map/ppermute | solution.py:50
  31.1 1.4 %collective-permute-done.11.refs_2_ = bf16[64,1024]{1,0:T(8,128)(2,1)S(1)} collective-permute-done((bf16[64,1024]{1,0:T(8,128)(2,1)S(1)}, bf16[64,1024]{1,0:T(8,128)(2,1)S(1)}, u32[]{:S(2)}, u32[]{:S(2)}) %collective-permute-start.11) | collective-permute-done | bytes 131104 | tf_op jit(solution)/shard_map/ppermute | solution.py:50
  32.6 2.1 %collective-permute-start.15 = (bf16[256,1024]{1,0:T(8,128)(2,1)S(1)}, bf16[256,1024]{1,0:T(8,128)(2,1)S(1)}, u32[]{:S(2)}, u32[]{:S(2)}) collective-permute-start(bf16[256,1024]{1,0:T(8,128)(2,1)S(1)} %pad_maximum_fusion), channel_id=1, source_target_pairs={{0,8},{8,0},{32,40},{40,32},{64,72},{72,64},{96,104},{104,96},{128... | collective-permute-start | bytes 1572872 | tf_op jit(solution)/shard_map/ppermute | solution.py:55
  34.7 0.8 %anchor_attention.2.refs_0_ = bf16[64,2048]{1,0:T(8,128)(2,1)S(1)} custom-call(bf16[64,4096]{1,0:T(8,128)(2,1)S(1)} %copy-done, f32[8,256,384]{2,1,0:T(8,128)S(1)} %own_attention.1.state_ref, bf16[64,1024]{1,0:T(8,128)(2,1)S(1)} %select_select_fusion.refs_0_, bf16[64,1024]{1,0:T(8,128)(2,1)S(1)} %collective-permute-done.10.refs_1_, ...), custom_call_target="tpu_custom_call" | custom-call | flops 134217728 | bytes 2097152 | tf_op jit(solution)/shard_map/anchor_attention/pallas_call | solution.py:189
  35.6 0.7 %collective-permute-done.15.refs_1_ = bf16[256,1024]{1,0:T(8,128)(2,1)S(1)} collective-permute-done((bf16[256,1024]{1,0:T(8,128)(2,1)S(1)}, bf16[256,1024]{1,0:T(8,128)(2,1)S(1)}, u32[]{:S(2)}, u32[]{:S(2)}) %collective-permute-start.15) | collective-permute-done | bytes 524320 | tf_op jit(solution)/shard_map/ppermute | solution.py:55
  36.3 1.6 %anchor_attention.3 = bf16[64,4096]{1,0:T(8,128)(2,1)} custom-call(bf16[64,4096]{1,0:T(8,128)(2,1)S(1)} %copy-done, f32[8,256,384]{2,1,0:T(8,128)S(1)} %own_attention.1.state_ref, bf16[64,2048]{1,0:T(8,128)(2,1)S(1)} %anchor_attention.2.refs_0_, bf16[256,1024]{1,0:T(8,128)(2,1)S(1)} %collective-permute-done.15.refs_1_), custom_call_target="tpu_custom_call" | custom-call | flops 134217728 | bytes 2097152 | tf_op jit(solution)/shard_map/anchor_attention/pallas_call | solution.py:189
  (23 shorter events, 0.8 us)
Async XLA Ops:
  0.0 27.6 %copy-start = (bf16[64,4096]{1,0:T(8,128)(2,1)S(1)}, bf16[64,4096]{1,0:T(8,128)(2,1)}, u32[]{:S(2)}) copy-start(bf16[64,4096]{1,0:T(8,128)(2,1)} %q_ref.5) | copy-start | bytes 1572868
  1.0 5.4 %collective-permute-start = (bf16[64,1024]{1,0:T(8,128)(2,1)S(1)}, bf16[64,1024]{1,0:T(8,128)(2,1)S(1)}, u32[]{:S(2)}, u32[]{:S(2)}) collective-permute-start(bf16[64,1024]{1,0:T(8,128)(2,1)S(1)} %pad_maximum_fusion.2), channel_id=1, source_target_pairs={{0,8},{1,9},{2,10},{3,11}} | collective-permute-start | bytes 393224 | tf_op jit(solution)/shard_map/ppermute | solution.py:209
  6.4 6.7 %collective-permute-start.1 = (bf16[64,1024]{1,0:T(8,128)(2,1)S(1)}, bf16[64,1024]{1,0:T(8,128)(2,1)S(1)}, u32[]{:S(2)}, u32[]{:S(2)}) collective-permute-start(bf16[64,1024]{1,0:T(8,128)(2,1)S(1)} %maximum_select_fusion), channel_id=1, source_target_pairs={{0,4},{8,12},{1,5},{9,13},{2,6},{10,14},{3,7},{11,15}} | collective-permute-start | bytes 393224 | tf_op jit(solution)/shard_map/ppermute | solution.py:70
  7.7 5.4 %collective-permute-start.2 = (bf16[64,1024]{1,0:T(8,128)(2,1)S(1)}, bf16[64,1024]{1,0:T(8,128)(2,1)S(1)}, u32[]{:S(2)}, u32[]{:S(2)}) collective-permute-start(bf16[64,1024]{1,0:T(8,128)(2,1)S(1)} %maximum_select_fusion), channel_id=1, source_target_pairs={{0,20},{8,28},{1,21},{9,29},{2,22},{10,30},{3,23},{11,31}} | collective-permute-start | bytes 393224 | tf_op jit(solution)/shard_map/ppermute | solution.py:70
  9.0 4.4 %collective-permute-start.3 = (bf16[64,1024]{1,0:T(8,128)(2,1)S(1)}, bf16[64,1024]{1,0:T(8,128)(2,1)S(1)}, u32[]{:S(2)}, u32[]{:S(2)}) collective-permute-start(bf16[64,1024]{1,0:T(8,128)(2,1)S(1)} %maximum_select_fusion), channel_id=1, source_target_pairs={{0,16},{8,24},{1,17},{9,25},{2,18},{10,26},{3,19},{11,27}} | collective-permute-start | bytes 393224 | tf_op jit(solution)/shard_map/ppermute | solution.py:70
  10.4 8.7 %collective-permute-start.6 = (bf16[64,2048]{1,0:T(8,128)(2,1)S(1)}, bf16[64,2048]{1,0:T(8,128)(2,1)S(1)}, u32[]{:S(2)}, u32[]{:S(2)}) collective-permute-start(bf16[64,2048]{1,0:T(8,128)(2,1)S(1)} %pad_maximum_fusion.1.own_ref), channel_id=1, source_target_pairs={{0,1},{8,9},{32,33},{40,41},{64,65},{72,73},{96,97},{104,105},{128... | collective-permute-start | bytes 786440 | tf_op jit(solution)/shard_map/ppermute | solution.py:50
  11.3 7.8 %collective-permute-start.7 = (bf16[64,2048]{1,0:T(8,128)(2,1)S(1)}, bf16[64,2048]{1,0:T(8,128)(2,1)S(1)}, u32[]{:S(2)}, u32[]{:S(2)}) collective-permute-start(bf16[64,2048]{1,0:T(8,128)(2,1)S(1)} %pad_maximum_fusion.1.own_ref), channel_id=1, source_target_pairs={{0,3},{8,11},{32,35},{40,43},{64,67},{72,75},{96,99},{104,107},{12... | collective-permute-start | bytes 786440 | tf_op jit(solution)/shard_map/ppermute | solution.py:50
  13.4 5.6 %collective-permute-start.4 = (bf16[64,1024]{1,0:T(8,128)(2,1)S(1)}, bf16[64,1024]{1,0:T(8,128)(2,1)S(1)}, u32[]{:S(2)}, u32[]{:S(2)}) collective-permute-start(bf16[64,1024]{1,0:T(8,128)(2,1)S(1)} %select_select_fusion.2), channel_id=1, source_target_pairs={{0,96},{8,104},{1,97},{9,105},{2,98},{10,106},{3,99},{11,107},{16,... | collective-permute-start | bytes 393224 | tf_op jit(solution)/shard_map/ppermute | solution.py:70
  14.8 4.3 %collective-permute-start.5 = (bf16[64,1024]{1,0:T(8,128)(2,1)S(1)}, bf16[64,1024]{1,0:T(8,128)(2,1)S(1)}, u32[]{:S(2)}, u32[]{:S(2)}) collective-permute-start(bf16[64,1024]{1,0:T(8,128)(2,1)S(1)} %select_select_fusion.2), channel_id=1, source_target_pairs={{0,192},{8,200},{1,193},{9,201},{2,194},{10,202},{3,195},{11,203},... | collective-permute-start | bytes 393224 | tf_op jit(solution)/shard_map/ppermute | solution.py:70
  19.1 4.9 %collective-permute-start.8 = (bf16[64,1024]{1,0:T(8,128)(2,1)S(1)}, bf16[64,1024]{1,0:T(8,128)(2,1)S(1)}, u32[]{:S(2)}, u32[]{:S(2)}) collective-permute-start(bf16[64,1024]{1,0:T(8,128)(2,1)S(1)} %select_select_fusion.1), channel_id=1, source_target_pairs={{0,32},{8,40},{1,33},{9,41},{2,34},{10,42},{3,35},{11,43},{16,48},... | collective-permute-start | bytes 393224 | tf_op jit(solution)/shard_map/ppermute | solution.py:70
  20.4 3.6 %collective-permute-start.9 = (bf16[64,1024]{1,0:T(8,128)(2,1)S(1)}, bf16[64,1024]{1,0:T(8,128)(2,1)S(1)}, u32[]{:S(2)}, u32[]{:S(2)}) collective-permute-start(bf16[64,1024]{1,0:T(8,128)(2,1)S(1)} %select_select_fusion.1), channel_id=1, source_target_pairs={{96,128},{104,136},{97,129},{105,137},{98,130},{106,138},{99,131},... | collective-permute-start | bytes 393224 | tf_op jit(solution)/shard_map/ppermute | solution.py:70
  21.1 6.5 %collective-permute-start.13 = (bf16[64,1024]{1,0:T(8,128)(2,1)S(1)}, bf16[64,1024]{1,0:T(8,128)(2,1)S(1)}, u32[]{:S(2)}, u32[]{:S(2)}) collective-permute-start(bf16[64,1024]{1,0:T(8,128)(2,1)S(1)} %slice.22), channel_id=1, source_target_pairs={{0,1},{8,9},{32,33},{40,41},{64,65},{72,73},{96,97},{104,105},{128... | collective-permute-start | bytes 393224 | tf_op jit(solution)/shard_map/ppermute | solution.py:50
  21.3 6.4 %collective-permute-start.14 = (bf16[64,1024]{1,0:T(8,128)(2,1)S(1)}, bf16[64,1024]{1,0:T(8,128)(2,1)S(1)}, u32[]{:S(2)}, u32[]{:S(2)}) collective-permute-start(bf16[64,1024]{1,0:T(8,128)(2,1)S(1)} %slice.23), channel_id=1, source_target_pairs={{0,3},{8,11},{32,35},{40,43},{64,67},{72,75},{96,99},{104,107},{12... | collective-permute-start | bytes 393224 | tf_op jit(solution)/shard_map/ppermute | solution.py:50
  24.0 7.1 %collective-permute-start.10 = (bf16[64,1024]{1,0:T(8,128)(2,1)S(1)}, bf16[64,1024]{1,0:T(8,128)(2,1)S(1)}, u32[]{:S(2)}, u32[]{:S(2)}) collective-permute-start(bf16[64,1024]{1,0:T(8,128)(2,1)S(1)} %select_select_fusion.refs_0_), channel_id=1, source_target_pairs={{0,2},{8,10},{32,34},{40,42},{64,66},{72,74},{96,98},{104,106},{12... | collective-permute-start | bytes 393224 | tf_op jit(solution)/shard_map/ppermute | solution.py:50
  25.0 7.5 %collective-permute-start.11 = (bf16[64,1024]{1,0:T(8,128)(2,1)S(1)}, bf16[64,1024]{1,0:T(8,128)(2,1)S(1)}, u32[]{:S(2)}, u32[]{:S(2)}) collective-permute-start(bf16[64,1024]{1,0:T(8,128)(2,1)S(1)} %select_select_fusion.refs_0_), channel_id=1, source_target_pairs={{0,1},{8,9},{32,33},{40,41},{64,65},{72,73},{96,97},{104,105},{128... | collective-permute-start | bytes 393224 | tf_op jit(solution)/shard_map/ppermute | solution.py:50
  25.8 6.8 %collective-permute-start.12 = (bf16[64,1024]{1,0:T(8,128)(2,1)S(1)}, bf16[64,1024]{1,0:T(8,128)(2,1)S(1)}, u32[]{:S(2)}, u32[]{:S(2)}) collective-permute-start(bf16[64,1024]{1,0:T(8,128)(2,1)S(1)} %select_select_fusion.refs_0_), channel_id=1, source_target_pairs={{0,3},{8,11},{32,35},{40,43},{64,67},{72,75},{96,99},{104,107},{12... | collective-permute-start | bytes 393224 | tf_op jit(solution)/shard_map/ppermute | solution.py:50
  32.6 3.7 %collective-permute-start.15 = (bf16[256,1024]{1,0:T(8,128)(2,1)S(1)}, bf16[256,1024]{1,0:T(8,128)(2,1)S(1)}, u32[]{:S(2)}, u32[]{:S(2)}) collective-permute-start(bf16[256,1024]{1,0:T(8,128)(2,1)S(1)} %pad_maximum_fusion), channel_id=1, source_target_pairs={{0,8},{8,0},{32,40},{40,32},{64,72},{72,64},{96,104},{104,96},{128... | collective-permute-start | bytes 1572872 | tf_op jit(solution)/shard_map/ppermute | solution.py:55

commit v5 on v4

--- a/solution.py
+++ b/solution.py
@@ -156,16 +156,17 @@
     blk, hd = lax.axis_index("blk"), lax.axis_index("hd")
     anchored = blk * 2 + (hd >> 2) > 0
     half = 1 - (blk & 1) if last else blk & 1
-    width = HALF * GROUP * HD
-    out_ref = refs[-1]
-    pieces = refs[1:-1] if last else refs[:-1]
+    out_ref, held_ref, sems = refs[-3:]
+    pieces = refs[1:-3] if last else refs[:-3]
+    width = GROUP * HD
+    copies = []
     for g in range(HALF):
         key = jnp.concatenate([r[:, g * HD : (g + 1) * HD] for r in pieces], axis=0)
         value = jnp.concatenate(
             [r[:, (HALF + g) * HD : (HALF + g + 1) * HD] for r in pieces], axis=0
         )
         head = half * HALF + g
-        start = pl.multiple_of(head * GROUP * HD, GROUP * HD)
+        start = pl.multiple_of(head * width, width)
         scores = raw_scores(stacked_queries(q_ref, start), key)
         scores = jnp.where(anchored, scores, -jnp.inf)
         state = state_ref[head]
@@ -176,19 +177,29 @@
         totals = jnp.sum(raised, axis=1, keepdims=True) + state[:, 2 * HD :] * keep
         mixture = jnp.dot(raised.astype(jnp.bfloat16), value, preferred_element_type=jnp.float32)
         result = ((mixture + state[:, :HD] * keep) / totals).astype(jnp.bfloat16)
-        base = start if last else g * GROUP * HD
         for i in range(GROUP):
-            out_ref[:, pl.ds(base + i * HD, HD)] = result[i * ROWS : (i + 1) * ROWS]
-    if last:
-        out_ref[:, pl.ds(pl.multiple_of((1 - half) * width, width), width)] = refs[0][...]
+            held_ref[g, :, i * HD : (i + 1) * HD] = result[i * ROWS : (i + 1) * ROWS]
+        copy = pltpu.make_async_copy(held_ref.at[g], out_ref.at[:, pl.ds(start, width)], sems.at[g])
+        copy.start()
+        copies.append(copy)
+    for copy in copies:
+        copy.wait()
 
 
 def anchor_attention(last, queries, own, *arrays):
     rows = GROUP * ROWS
-    width = H * HD if last else H * HD // 2
+    near = pl.BlockSpec(memory_space=pltpu.VMEM)
+    far = pl.BlockSpec(memory_space=pl.ANY)
     return pl.pallas_call(
         functools.partial(anchor_kernel, last),
-        out_shape=jax.ShapeDtypeStruct((ROWS, width), jnp.bfloat16),
+        out_shape=jax.ShapeDtypeStruct((ROWS, H * HD), jnp.bfloat16),
+        in_specs=[near, near] + [far if last and i == 0 else near for i in range(len(arrays))],
+        out_specs=far,
+        input_output_aliases={2: 0} if last else {},
+        scratch_shapes=[
+            pltpu.VMEM((HALF, ROWS, GROUP * HD), jnp.bfloat16),
+            pltpu.SemaphoreType.DMA((HALF,)),
+        ],
         cost_estimate=pl.CostEstimate(
             flops=4 * HALF * rows * BLK * HD,
             bytes_accessed=2 << 20,

time: 38.1 us -> 38 us (level)
  waiting for transfers between devices: 11.7 us -> 11 us
  Pallas kernels: 3.61 us -> 4.15 us
    ppermute x1, waiting for transfers between devices: 0.69 us -> 0.02 us  [to_other_core(): return lax.ppermute(array, AXES, pairs)]
    pallas_call x2, Pallas kernels: 2.48 us -> 3.01 us  [anchor_attention(): pl.pallas_call(functools.partial(anchor_kernel, last), out_shape=jax.Shap...]
  transfers between devices with their start and end apart: 16 -> 16, of which waited for: 7 -> 6; matrix products, arithmetic and copies ran while one was open for 0% -> 0% of each run, Pallas kernels for 5% -> 7%
where the time goes in v5:
time: 38 us; the launch traced here: 37.8 us
  starting transfers between devices  21.3 us (56%)
  waiting for transfers between devices  11 us (29%)
  Pallas kernels  4.15 us (11%)
  local copies, waits for them, and re-layouts  1.03 us (3%)
    ppermute x7, starting transfers between devices, along_y(): return lax.ppermute(array, AXES, pairs)  9.24 us
    ppermute x7, starting transfers between devices, spread(): came.append((lax.ppermute(piece, AXES, pairs), [b for _, b in moves]))  8.62 us
    ppermute x7, waiting for transfers between devices, along_y(): return lax.ppermute(array, AXES, pairs)  6.61 us
    ppermute x1, waiting for transfers between devices, shards(): lax.ppermute(high, AXES, [(place(0, y, 0, 0), place(0, y, 0, 1)) for y in...  4.05 us
    pallas_call x2, Pallas kernels, anchor_attention(): pl.pallas_call(functools.partial(anchor_kernel, last), out_shape=jax.Shap...  3.01 us
    ppermute x1, starting transfers between devices, to_other_core(): return lax.ppermute(array, AXES, pairs)  2.11 us
    ppermute x1, starting transfers between devices, shards(): lax.ppermute(high, AXES, [(place(0, y, 0, 0), place(0, y, 0, 1)) for y in...  1.29 us
    pallas_call x1, Pallas kernels, own_attention(): pl.pallas_call(own_kernel, out_shape=jax.ShapeDtypeStruct((KV, rows, 3 *...  1.13 us
  transfers between devices with their start and end apart: 16, of which 6 were waited for; matrix products, arithmetic and copies ran while one was open for 0% of the time, Pallas kernels for 7%

profile of v5, /device:TPU:1, one launch (start us, length us, event | category | flops | bytes accessed | tf_op | source)
XLA Modules:
  0.0 37.8 jit_solution(17385001543734346221)
XLA Ops:
  0.0 1.0 %fusion = (bf16[64,512]{1,0:T(8,128)(2,1)S(1)}, bf16[64,512]{1,0:T(8,128)(2,1)S(1)}, bf16[64,512]{1,0:T(8,128)(2,1)S(1)}, bf16[64,512]{1,0:T(8,128)(2,1)S(1)}) fusion(bf16[64,1024]{1,0:T(8,128)(2,1)} %param.4, bf16[64,1024]{1,0:T(8,128)(2,1)} %param.5), kind=kLoop, calls=%fused_computation.7 | loop fusion | bytes 524288 | tf_op jit(solution)/shard_map/slice | solution.py:216
  1.0 1.3 %collective-permute-start = (bf16[64,1024]{1,0:T(8,128)(2,1)S(1)}, bf16[64,1024]{1,0:T(8,128)(2,1)S(1)}, u32[]{:S(2)}, u32[]{:S(2)}) collective-permute-start(bf16[64,1024]{1,0:T(8,128)(2,1)S(1)} %pad_maximum_fusion.2), channel_id=1, source_target_pairs={{0,8},{1,9},{2,10},{3,11}} | collective-permute-start | bytes 393224 | tf_op jit(solution)/shard_map/ppermute | solution.py:220
  2.3 4.1 %collective-permute-done = bf16[64,1024]{1,0:T(8,128)(2,1)S(1)} collective-permute-done((bf16[64,1024]{1,0:T(8,128)(2,1)S(1)}, bf16[64,1024]{1,0:T(8,128)(2,1)S(1)}, u32[]{:S(2)}, u32[]{:S(2)}) %collective-permute-start) | collective-permute-done | bytes 131104 | tf_op jit(solution)/shard_map/ppermute | solution.py:220
  6.4 1.3 %collective-permute-start.1 = (bf16[64,1024]{1,0:T(8,128)(2,1)S(1)}, bf16[64,1024]{1,0:T(8,128)(2,1)S(1)}, u32[]{:S(2)}, u32[]{:S(2)}) collective-permute-start(bf16[64,1024]{1,0:T(8,128)(2,1)S(1)} %maximum_select_fusion), channel_id=1, source_target_pairs={{0,4},{8,12},{1,5},{9,13},{2,6},{10,14},{3,7},{11,15}} | collective-permute-start | bytes 393224 | tf_op jit(solution)/shard_map/ppermute | solution.py:70
  7.7 1.3 %collective-permute-start.2 = (bf16[64,1024]{1,0:T(8,128)(2,1)S(1)}, bf16[64,1024]{1,0:T(8,128)(2,1)S(1)}, u32[]{:S(2)}, u32[]{:S(2)}) collective-permute-start(bf16[64,1024]{1,0:T(8,128)(2,1)S(1)} %maximum_select_fusion), channel_id=1, source_target_pairs={{0,20},{8,28},{1,21},{9,29},{2,22},{10,30},{3,23},{11,31}} | collective-permute-start | bytes 393224 | tf_op jit(solution)/shard_map/ppermute | solution.py:70
  9.0 1.3 %collective-permute-start.3 = (bf16[64,1024]{1,0:T(8,128)(2,1)S(1)}, bf16[64,1024]{1,0:T(8,128)(2,1)S(1)}, u32[]{:S(2)}, u32[]{:S(2)}) collective-permute-start(bf16[64,1024]{1,0:T(8,128)(2,1)S(1)} %maximum_select_fusion), channel_id=1, source_target_pairs={{0,16},{8,24},{1,17},{9,25},{2,18},{10,26},{3,19},{11,27}} | collective-permute-start | bytes 393224 | tf_op jit(solution)/shard_map/ppermute | solution.py:70
  10.4 0.9 %collective-permute-start.6 = (bf16[64,2048]{1,0:T(8,128)(2,1)S(1)}, bf16[64,2048]{1,0:T(8,128)(2,1)S(1)}, u32[]{:S(2)}, u32[]{:S(2)}) collective-permute-start(bf16[64,2048]{1,0:T(8,128)(2,1)S(1)} %pad_maximum_fusion.1.own_ref), channel_id=1, source_target_pairs={{0,1},{8,9},{32,33},{40,41},{64,65},{72,73},{96,97},{104,105},{128... | collective-permute-start | bytes 786440 | tf_op jit(solution)/shard_map/ppermute | solution.py:50
  11.3 1.9 %collective-permute-start.7 = (bf16[64,2048]{1,0:T(8,128)(2,1)S(1)}, bf16[64,2048]{1,0:T(8,128)(2,1)S(1)}, u32[]{:S(2)}, u32[]{:S(2)}) collective-permute-start(bf16[64,2048]{1,0:T(8,128)(2,1)S(1)} %pad_maximum_fusion.1.own_ref), channel_id=1, source_target_pairs={{0,3},{8,11},{32,35},{40,43},{64,67},{72,75},{96,99},{104,107},{12... | collective-permute-start | bytes 786440 | tf_op jit(solution)/shard_map/ppermute | solution.py:50
  13.1 0.3 collective-permute-done.3
  13.4 1.3 %collective-permute-start.4 = (bf16[64,1024]{1,0:T(8,128)(2,1)S(1)}, bf16[64,1024]{1,0:T(8,128)(2,1)S(1)}, u32[]{:S(2)}, u32[]{:S(2)}) collective-permute-start(bf16[64,1024]{1,0:T(8,128)(2,1)S(1)} %select_select_fusion.2), channel_id=1, source_target_pairs={{0,96},{8,104},{1,97},{9,105},{2,98},{10,106},{3,99},{11,107},{16,... | collective-permute-start | bytes 393224 | tf_op jit(solution)/shard_map/ppermute | solution.py:70
  14.8 1.5 %collective-permute-start.5 = (bf16[64,1024]{1,0:T(8,128)(2,1)S(1)}, bf16[64,1024]{1,0:T(8,128)(2,1)S(1)}, u32[]{:S(2)}, u32[]{:S(2)}) collective-permute-start(bf16[64,1024]{1,0:T(8,128)(2,1)S(1)} %select_select_fusion.2), channel_id=1, source_target_pairs={{0,192},{8,200},{1,193},{9,201},{2,194},{10,202},{3,195},{11,203},... | collective-permute-start | bytes 393224 | tf_op jit(solution)/shard_map/ppermute | solution.py:70
  16.2 2.8 %collective-permute-done.6.near_ref = bf16[64,2048]{1,0:T(8,128)(2,1)S(1)} collective-permute-done((bf16[64,2048]{1,0:T(8,128)(2,1)S(1)}, bf16[64,2048]{1,0:T(8,128)(2,1)S(1)}, u32[]{:S(2)}, u32[]{:S(2)}) %collective-permute-start.6) | collective-permute-done | bytes 262176 | tf_op jit(solution)/shard_map/ppermute | solution.py:50
  19.1 1.3 %collective-permute-start.8 = (bf16[64,1024]{1,0:T(8,128)(2,1)S(1)}, bf16[64,1024]{1,0:T(8,128)(2,1)S(1)}, u32[]{:S(2)}, u32[]{:S(2)}) collective-permute-start(bf16[64,1024]{1,0:T(8,128)(2,1)S(1)} %select_select_fusion.1), channel_id=1, source_target_pairs={{0,32},{8,40},{1,33},{9,41},{2,34},{10,42},{3,35},{11,43},{16,48},... | collective-permute-start | bytes 393224 | tf_op jit(solution)/shard_map/ppermute | solution.py:70
  20.4 0.7 %collective-permute-start.9 = (bf16[64,1024]{1,0:T(8,128)(2,1)S(1)}, bf16[64,1024]{1,0:T(8,128)(2,1)S(1)}, u32[]{:S(2)}, u32[]{:S(2)}) collective-permute-start(bf16[64,1024]{1,0:T(8,128)(2,1)S(1)} %select_select_fusion.1), channel_id=1, source_target_pairs={{96,128},{104,136},{97,129},{105,137},{98,130},{106,138},{99,131},... | collective-permute-start | bytes 393224 | tf_op jit(solution)/shard_map/ppermute | solution.py:70
  21.3 2.7 %collective-permute-start.14 = (bf16[64,1024]{1,0:T(8,128)(2,1)S(1)}, bf16[64,1024]{1,0:T(8,128)(2,1)S(1)}, u32[]{:S(2)}, u32[]{:S(2)}) collective-permute-start(bf16[64,1024]{1,0:T(8,128)(2,1)S(1)} %slice.23), channel_id=1, source_target_pairs={{0,3},{8,11},{32,35},{40,43},{64,67},{72,75},{96,99},{104,107},{12... | collective-permute-start | bytes 393224 | tf_op jit(solution)/shard_map/ppermute | solution.py:50
  24.0 1.0 %collective-permute-start.10 = (bf16[64,1024]{1,0:T(8,128)(2,1)S(1)}, bf16[64,1024]{1,0:T(8,128)(2,1)S(1)}, u32[]{:S(2)}, u32[]{:S(2)}) collective-permute-start(bf16[64,1024]{1,0:T(8,128)(2,1)S(1)} %select_select_fusion.refs_0_), channel_id=1, source_target_pairs={{0,2},{8,10},{32,34},{40,42},{64,66},{72,74},{96,98},{104,106},{12... | collective-permute-start | bytes 393224 | tf_op jit(solution)/shard_map/ppermute | solution.py:50
  25.0 0.8 %collective-permute-start.11 = (bf16[64,1024]{1,0:T(8,128)(2,1)S(1)}, bf16[64,1024]{1,0:T(8,128)(2,1)S(1)}, u32[]{:S(2)}, u32[]{:S(2)}) collective-permute-start(bf16[64,1024]{1,0:T(8,128)(2,1)S(1)} %select_select_fusion.refs_0_), channel_id=1, source_target_pairs={{0,1},{8,9},{32,33},{40,41},{64,65},{72,73},{96,97},{104,105},{128... | collective-permute-start | bytes 393224 | tf_op jit(solution)/shard_map/ppermute | solution.py:50
  25.8 1.9 %collective-permute-start.12 = (bf16[64,1024]{1,0:T(8,128)(2,1)S(1)}, bf16[64,1024]{1,0:T(8,128)(2,1)S(1)}, u32[]{:S(2)}, u32[]{:S(2)}) collective-permute-start(bf16[64,1024]{1,0:T(8,128)(2,1)S(1)} %select_select_fusion.refs_0_), channel_id=1, source_target_pairs={{0,3},{8,11},{32,35},{40,43},{64,67},{72,75},{96,99},{104,107},{12... | collective-permute-start | bytes 393224 | tf_op jit(solution)/shard_map/ppermute | solution.py:50
  27.6 1.1 %own_attention.1.state_ref = f32[8,256,384]{2,1,0:T(8,128)S(1)} custom-call(bf16[64,4096]{1,0:T(8,128)(2,1)S(1)} %copy-done, bf16[64,2048]{1,0:T(8,128)(2,1)S(1)} %pad_maximum_fusion.1.own_ref, bf16[64,2048]{1,0:T(8,128)(2,1)S(1)} %collective-permute-done.6.near_ref, bf16[64,2048]{1,0:T(8,128)(2,1)S(1)} %collective-permute-done.7.far_ref, ...), custom_call_target="tpu_custom_call" | custom-call | flops 268435456 | bytes 4194304 | tf_op jit(solution)/shard_map/own_attention/pallas_call | solution.py:144
  28.8 2.3 %collective-permute-done.10.refs_1_ = bf16[64,1024]{1,0:T(8,128)(2,1)S(1)} collective-permute-done((bf16[64,1024]{1,0:T(8,128)(2,1)S(1)}, bf16[64,1024]{1,0:T(8,128)(2,1)S(1)}, u32[]{:S(2)}, u32[]{:S(2)}) %collective-permute-start.10) | collective-permute-done | bytes 131104 | tf_op jit(solution)/shard_map/ppermute | solution.py:50
  31.1 1.4 %collective-permute-done.11.refs_2_ = bf16[64,1024]{1,0:T(8,128)(2,1)S(1)} collective-permute-done((bf16[64,1024]{1,0:T(8,128)(2,1)S(1)}, bf16[64,1024]{1,0:T(8,128)(2,1)S(1)}, u32[]{:S(2)}, u32[]{:S(2)}) %collective-permute-start.11) | collective-permute-done | bytes 131104 | tf_op jit(solution)/shard_map/ppermute | solution.py:50
  32.6 2.1 %collective-permute-start.15 = (bf16[256,1024]{1,0:T(8,128)(2,1)S(1)}, bf16[256,1024]{1,0:T(8,128)(2,1)S(1)}, u32[]{:S(2)}, u32[]{:S(2)}) collective-permute-start(bf16[256,1024]{1,0:T(8,128)(2,1)S(1)} %pad_maximum_fusion), channel_id=1, source_target_pairs={{0,8},{8,0},{32,40},{40,32},{64,72},{72,64},{96,104},{104,96},{128... | collective-permute-start | bytes 1572872 | tf_op jit(solution)/shard_map/ppermute | solution.py:55
  34.7 1.5 %anchor_attention.2.refs_0_ = bf16[64,4096]{1,0:T(8,128)(2,1)} custom-call(bf16[64,4096]{1,0:T(8,128)(2,1)S(1)} %copy-done, f32[8,256,384]{2,1,0:T(8,128)S(1)} %own_attention.1.state_ref, bf16[64,1024]{1,0:T(8,128)(2,1)S(1)} %select_select_fusion.refs_0_, bf16[64,1024]{1,0:T(8,128)(2,1)S(1)} %collective-permute-done.10.refs_1_, ...), custom_call_target="tpu_custom_call" | custom-call | flops 134217728 | bytes 2097152 | tf_op jit(solution)/shard_map/anchor_attention/pallas_call | solution.py:193
  36.3 1.5 %anchor_attention.3 = bf16[64,4096]{1,0:T(8,128)(2,1)} custom-call(bf16[64,4096]{1,0:T(8,128)(2,1)S(1)} %copy-done, f32[8,256,384]{2,1,0:T(8,128)S(1)} %own_attention.1.state_ref, bf16[64,4096]{1,0:T(8,128)(2,1)} %anchor_attention.2.refs_0_, bf16[256,1024]{1,0:T(8,128)(2,1)S(1)} %collective-permute-done.15.refs_1_), custom_call_target="tpu_custom_call", output_to_operand_aliasing={{}: (2, {})} | custom-call | flops 134217728 | bytes 2097152 | tf_op jit(solution)/shard_map/anchor_attention/pallas_call | solution.py:193
  (23 shorter events, 0.5 us)
Async XLA Ops:
  0.0 27.6 %copy-start = (bf16[64,4096]{1,0:T(8,128)(2,1)S(1)}, bf16[64,4096]{1,0:T(8,128)(2,1)}, u32[]{:S(2)}) copy-start(bf16[64,4096]{1,0:T(8,128)(2,1)} %q_ref.5) | copy-start | bytes 1572868
  1.0 5.4 %collective-permute-start = (bf16[64,1024]{1,0:T(8,128)(2,1)S(1)}, bf16[64,1024]{1,0:T(8,128)(2,1)S(1)}, u32[]{:S(2)}, u32[]{:S(2)}) collective-permute-start(bf16[64,1024]{1,0:T(8,128)(2,1)S(1)} %pad_maximum_fusion.2), channel_id=1, source_target_pairs={{0,8},{1,9},{2,10},{3,11}} | collective-permute-start | bytes 393224 | tf_op jit(solution)/shard_map/ppermute | solution.py:220
  6.4 6.7 %collective-permute-start.1 = (bf16[64,1024]{1,0:T(8,128)(2,1)S(1)}, bf16[64,1024]{1,0:T(8,128)(2,1)S(1)}, u32[]{:S(2)}, u32[]{:S(2)}) collective-permute-start(bf16[64,1024]{1,0:T(8,128)(2,1)S(1)} %maximum_select_fusion), channel_id=1, source_target_pairs={{0,4},{8,12},{1,5},{9,13},{2,6},{10,14},{3,7},{11,15}} | collective-permute-start | bytes 393224 | tf_op jit(solution)/shard_map/ppermute | solution.py:70
  7.7 5.4 %collective-permute-start.2 = (bf16[64,1024]{1,0:T(8,128)(2,1)S(1)}, bf16[64,1024]{1,0:T(8,128)(2,1)S(1)}, u32[]{:S(2)}, u32[]{:S(2)}) collective-permute-start(bf16[64,1024]{1,0:T(8,128)(2,1)S(1)} %maximum_select_fusion), channel_id=1, source_target_pairs={{0,20},{8,28},{1,21},{9,29},{2,22},{10,30},{3,23},{11,31}} | collective-permute-start | bytes 393224 | tf_op jit(solution)/shard_map/ppermute | solution.py:70
  9.0 4.4 %collective-permute-start.3 = (bf16[64,1024]{1,0:T(8,128)(2,1)S(1)}, bf16[64,1024]{1,0:T(8,128)(2,1)S(1)}, u32[]{:S(2)}, u32[]{:S(2)}) collective-permute-start(bf16[64,1024]{1,0:T(8,128)(2,1)S(1)} %maximum_select_fusion), channel_id=1, source_target_pairs={{0,16},{8,24},{1,17},{9,25},{2,18},{10,26},{3,19},{11,27}} | collective-permute-start | bytes 393224 | tf_op jit(solution)/shard_map/ppermute | solution.py:70
  10.4 8.7 %collective-permute-start.6 = (bf16[64,2048]{1,0:T(8,128)(2,1)S(1)}, bf16[64,2048]{1,0:T(8,128)(2,1)S(1)}, u32[]{:S(2)}, u32[]{:S(2)}) collective-permute-start(bf16[64,2048]{1,0:T(8,128)(2,1)S(1)} %pad_maximum_fusion.1.own_ref), channel_id=1, source_target_pairs={{0,1},{8,9},{32,33},{40,41},{64,65},{72,73},{96,97},{104,105},{128... | collective-permute-start | bytes 786440 | tf_op jit(solution)/shard_map/ppermute | solution.py:50
  11.3 7.8 %collective-permute-start.7 = (bf16[64,2048]{1,0:T(8,128)(2,1)S(1)}, bf16[64,2048]{1,0:T(8,128)(2,1)S(1)}, u32[]{:S(2)}, u32[]{:S(2)}) collective-permute-start(bf16[64,2048]{1,0:T(8,128)(2,1)S(1)} %pad_maximum_fusion.1.own_ref), channel_id=1, source_target_pairs={{0,3},{8,11},{32,35},{40,43},{64,67},{72,75},{96,99},{104,107},{12... | collective-permute-start | bytes 786440 | tf_op jit(solution)/shard_map/ppermute | solution.py:50
  13.4 5.6 %collective-permute-start.4 = (bf16[64,1024]{1,0:T(8,128)(2,1)S(1)}, bf16[64,1024]{1,0:T(8,128)(2,1)S(1)}, u32[]{:S(2)}, u32[]{:S(2)}) collective-permute-start(bf16[64,1024]{1,0:T(8,128)(2,1)S(1)} %select_select_fusion.2), channel_id=1, source_target_pairs={{0,96},{8,104},{1,97},{9,105},{2,98},{10,106},{3,99},{11,107},{16,... | collective-permute-start | bytes 393224 | tf_op jit(solution)/shard_map/ppermute | solution.py:70
  14.8 4.3 %collective-permute-start.5 = (bf16[64,1024]{1,0:T(8,128)(2,1)S(1)}, bf16[64,1024]{1,0:T(8,128)(2,1)S(1)}, u32[]{:S(2)}, u32[]{:S(2)}) collective-permute-start(bf16[64,1024]{1,0:T(8,128)(2,1)S(1)} %select_select_fusion.2), channel_id=1, source_target_pairs={{0,192},{8,200},{1,193},{9,201},{2,194},{10,202},{3,195},{11,203},... | collective-permute-start | bytes 393224 | tf_op jit(solution)/shard_map/ppermute | solution.py:70
  19.1 4.9 %collective-permute-start.8 = (bf16[64,1024]{1,0:T(8,128)(2,1)S(1)}, bf16[64,1024]{1,0:T(8,128)(2,1)S(1)}, u32[]{:S(2)}, u32[]{:S(2)}) collective-permute-start(bf16[64,1024]{1,0:T(8,128)(2,1)S(1)} %select_select_fusion.1), channel_id=1, source_target_pairs={{0,32},{8,40},{1,33},{9,41},{2,34},{10,42},{3,35},{11,43},{16,48},... | collective-permute-start | bytes 393224 | tf_op jit(solution)/shard_map/ppermute | solution.py:70
  20.4 3.6 %collective-permute-start.9 = (bf16[64,1024]{1,0:T(8,128)(2,1)S(1)}, bf16[64,1024]{1,0:T(8,128)(2,1)S(1)}, u32[]{:S(2)}, u32[]{:S(2)}) collective-permute-start(bf16[64,1024]{1,0:T(8,128)(2,1)S(1)} %select_select_fusion.1), channel_id=1, source_target_pairs={{96,128},{104,136},{97,129},{105,137},{98,130},{106,138},{99,131},... | collective-permute-start | bytes 393224 | tf_op jit(solution)/shard_map/ppermute | solution.py:70
  21.1 6.5 %collective-permute-start.13 = (bf16[64,1024]{1,0:T(8,128)(2,1)S(1)}, bf16[64,1024]{1,0:T(8,128)(2,1)S(1)}, u32[]{:S(2)}, u32[]{:S(2)}) collective-permute-start(bf16[64,1024]{1,0:T(8,128)(2,1)S(1)} %slice.22), channel_id=1, source_target_pairs={{0,1},{8,9},{32,33},{40,41},{64,65},{72,73},{96,97},{104,105},{128... | collective-permute-start | bytes 393224 | tf_op jit(solution)/shard_map/ppermute | solution.py:50
  21.3 6.4 %collective-permute-start.14 = (bf16[64,1024]{1,0:T(8,128)(2,1)S(1)}, bf16[64,1024]{1,0:T(8,128)(2,1)S(1)}, u32[]{:S(2)}, u32[]{:S(2)}) collective-permute-start(bf16[64,1024]{1,0:T(8,128)(2,1)S(1)} %slice.23), channel_id=1, source_target_pairs={{0,3},{8,11},{32,35},{40,43},{64,67},{72,75},{96,99},{104,107},{12... | collective-permute-start | bytes 393224 | tf_op jit(solution)/shard_map/ppermute | solution.py:50
  24.0 7.1 %collective-permute-start.10 = (bf16[64,1024]{1,0:T(8,128)(2,1)S(1)}, bf16[64,1024]{1,0:T(8,128)(2,1)S(1)}, u32[]{:S(2)}, u32[]{:S(2)}) collective-permute-start(bf16[64,1024]{1,0:T(8,128)(2,1)S(1)} %select_select_fusion.refs_0_), channel_id=1, source_target_pairs={{0,2},{8,10},{32,34},{40,42},{64,66},{72,74},{96,98},{104,106},{12... | collective-permute-start | bytes 393224 | tf_op jit(solution)/shard_map/ppermute | solution.py:50
  25.0 7.5 %collective-permute-start.11 = (bf16[64,1024]{1,0:T(8,128)(2,1)S(1)}, bf16[64,1024]{1,0:T(8,128)(2,1)S(1)}, u32[]{:S(2)}, u32[]{:S(2)}) collective-permute-start(bf16[64,1024]{1,0:T(8,128)(2,1)S(1)} %select_select_fusion.refs_0_), channel_id=1, source_target_pairs={{0,1},{8,9},{32,33},{40,41},{64,65},{72,73},{96,97},{104,105},{128... | collective-permute-start | bytes 393224 | tf_op jit(solution)/shard_map/ppermute | solution.py:50
  25.8 6.8 %collective-permute-start.12 = (bf16[64,1024]{1,0:T(8,128)(2,1)S(1)}, bf16[64,1024]{1,0:T(8,128)(2,1)S(1)}, u32[]{:S(2)}, u32[]{:S(2)}) collective-permute-start(bf16[64,1024]{1,0:T(8,128)(2,1)S(1)} %select_select_fusion.refs_0_), channel_id=1, source_target_pairs={{0,3},{8,11},{32,35},{40,43},{64,67},{72,75},{96,99},{104,107},{12... | collective-permute-start | bytes 393224 | tf_op jit(solution)/shard_map/ppermute | solution.py:50
  32.6 3.7 %collective-permute-start.15 = (bf16[256,1024]{1,0:T(8,128)(2,1)S(1)}, bf16[256,1024]{1,0:T(8,128)(2,1)S(1)}, u32[]{:S(2)}, u32[]{:S(2)}) collective-permute-start(bf16[256,1024]{1,0:T(8,128)(2,1)S(1)} %pad_maximum_fusion), channel_id=1, source_target_pairs={{0,8},{8,0},{32,40},{40,32},{64,72},{72,64},{96,104},{104,96},{128... | collective-permute-start | bytes 1572872 | tf_op jit(solution)/shard_map/ppermute | solution.py:55

commit v6 on v5

--- a/solution.py
+++ b/solution.py
@@ -85,8 +85,8 @@
     (by(1, 0), by(3, 0), by(2, 0)),
     (by(0, 3), by(0, 6)),
     (
-        lambda x, z: [(x, {3: 4, 6: 5}[z])] if z else [],
-        lambda x, z: [(x, {0: 1, 3: 2, 6: 7}[z])],
+        lambda x, z: [(x, {0: 1, 3: 4, 6: 7}[z])] if z in {0: 1, 3: 4, 6: 7} else [],
+        lambda x, z: [(x, {3: 2, 6: 5}[z])] if z in {3: 2, 6: 5} else [],
     ),
 )
 

time: 38 us -> 38 us (level)
  no operation moved by 1% of the time
where the time goes in v6:
time: 38 us; the launch traced here: 37.8 us
  starting transfers between devices  21.5 us (57%)
  waiting for transfers between devices  10.7 us (28%)
  Pallas kernels  4.15 us (11%)
  local copies, waits for them, and re-layouts  1.03 us (3%)
    ppermute x7, starting transfers between devices, along_y(): return lax.ppermute(array, AXES, pairs)  9.24 us
    ppermute x7, starting transfers between devices, spread(): came.append((lax.ppermute(piece, AXES, pairs), [b for _, b in moves]))  8.62 us
    ppermute x7, waiting for transfers between devices, along_y(): return lax.ppermute(array, AXES, pairs)  6.34 us
    ppermute x1, waiting for transfers between devices, shards(): lax.ppermute(high, AXES, [(place(0, y, 0, 0), place(0, y, 0, 1)) for y in...  4.05 us
    pallas_call x2, Pallas kernels, anchor_attention(): pl.pallas_call(functools.partial(anchor_kernel, last), out_shape=jax.Shap...  3.01 us
    ppermute x1, starting transfers between devices, to_other_core(): return lax.ppermute(array, AXES, pairs)  2.39 us
    ppermute x1, starting transfers between devices, shards(): lax.ppermute(high, AXES, [(place(0, y, 0, 0), place(0, y, 0, 1)) for y in...  1.29 us
    pallas_call x1, Pallas kernels, own_attention(): pl.pallas_call(own_kernel, out_shape=jax.ShapeDtypeStruct((KV, rows, 3 *...  1.13 us
  transfers between devices with their start and end apart: 16, of which 6 were waited for; matrix products, arithmetic and copies ran while one was open for 0% of the time, Pallas kernels for 7%

profile of v6, /device:TPU:1, one launch (start us, length us, event | category | flops | bytes accessed | tf_op | source)
XLA Modules:
  0.0 37.8 jit_solution(16449830089680477953)
XLA Ops:
  0.0 1.0 %fusion = (bf16[64,512]{1,0:T(8,128)(2,1)S(1)}, bf16[64,512]{1,0:T(8,128)(2,1)S(1)}, bf16[64,512]{1,0:T(8,128)(2,1)S(1)}, bf16[64,512]{1,0:T(8,128)(2,1)S(1)}) fusion(bf16[64,1024]{1,0:T(8,128)(2,1)} %param.4, bf16[64,1024]{1,0:T(8,128)(2,1)} %param.5), kind=kLoop, calls=%fused_computation.7 | loop fusion | bytes 524288 | tf_op jit(solution)/shard_map/slice | solution.py:216
  1.0 1.3 %collective-permute-start = (bf16[64,1024]{1,0:T(8,128)(2,1)S(1)}, bf16[64,1024]{1,0:T(8,128)(2,1)S(1)}, u32[]{:S(2)}, u32[]{:S(2)}) collective-permute-start(bf16[64,1024]{1,0:T(8,128)(2,1)S(1)} %pad_maximum_fusion.2), channel_id=1, source_target_pairs={{0,8},{1,9},{2,10},{3,11}} | collective-permute-start | bytes 393224 | tf_op jit(solution)/shard_map/ppermute | solution.py:220
  2.3 4.1 %collective-permute-done = bf16[64,1024]{1,0:T(8,128)(2,1)S(1)} collective-permute-done((bf16[64,1024]{1,0:T(8,128)(2,1)S(1)}, bf16[64,1024]{1,0:T(8,128)(2,1)S(1)}, u32[]{:S(2)}, u32[]{:S(2)}) %collective-permute-start) | collective-permute-done | bytes 131104 | tf_op jit(solution)/shard_map/ppermute | solution.py:220
  6.4 1.3 %collective-permute-start.1 = (bf16[64,1024]{1,0:T(8,128)(2,1)S(1)}, bf16[64,1024]{1,0:T(8,128)(2,1)S(1)}, u32[]{:S(2)}, u32[]{:S(2)}) collective-permute-start(bf16[64,1024]{1,0:T(8,128)(2,1)S(1)} %maximum_select_fusion), channel_id=1, source_target_pairs={{0,4},{8,12},{1,5},{9,13},{2,6},{10,14},{3,7},{11,15}} | collective-permute-start | bytes 393224 | tf_op jit(solution)/shard_map/ppermute | solution.py:70
  7.7 1.3 %collective-permute-start.2 = (bf16[64,1024]{1,0:T(8,128)(2,1)S(1)}, bf16[64,1024]{1,0:T(8,128)(2,1)S(1)}, u32[]{:S(2)}, u32[]{:S(2)}) collective-permute-start(bf16[64,1024]{1,0:T(8,128)(2,1)S(1)} %maximum_select_fusion), channel_id=1, source_target_pairs={{0,20},{8,28},{1,21},{9,29},{2,22},{10,30},{3,23},{11,31}} | collective-permute-start | bytes 393224 | tf_op jit(solution)/shard_map/ppermute | solution.py:70
  9.0 1.3 %collective-permute-start.3 = (bf16[64,1024]{1,0:T(8,128)(2,1)S(1)}, bf16[64,1024]{1,0:T(8,128)(2,1)S(1)}, u32[]{:S(2)}, u32[]{:S(2)}) collective-permute-start(bf16[64,1024]{1,0:T(8,128)(2,1)S(1)} %maximum_select_fusion), channel_id=1, source_target_pairs={{0,16},{8,24},{1,17},{9,25},{2,18},{10,26},{3,19},{11,27}} | collective-permute-start | bytes 393224 | tf_op jit(solution)/shard_map/ppermute | solution.py:70
  10.4 0.9 %collective-permute-start.6 = (bf16[64,2048]{1,0:T(8,128)(2,1)S(1)}, bf16[64,2048]{1,0:T(8,128)(2,1)S(1)}, u32[]{:S(2)}, u32[]{:S(2)}) collective-permute-start(bf16[64,2048]{1,0:T(8,128)(2,1)S(1)} %pad_maximum_fusion.1.own_ref), channel_id=1, source_target_pairs={{0,1},{8,9},{32,33},{40,41},{64,65},{72,73},{96,97},{104,105},{128... | collective-permute-start | bytes 786440 | tf_op jit(solution)/shard_map/ppermute | solution.py:50
  11.3 1.9 %collective-permute-start.7 = (bf16[64,2048]{1,0:T(8,128)(2,1)S(1)}, bf16[64,2048]{1,0:T(8,128)(2,1)S(1)}, u32[]{:S(2)}, u32[]{:S(2)}) collective-permute-start(bf16[64,2048]{1,0:T(8,128)(2,1)S(1)} %pad_maximum_fusion.1.own_ref), channel_id=1, source_target_pairs={{0,3},{8,11},{32,35},{40,43},{64,67},{72,75},{96,99},{104,107},{12... | collective-permute-start | bytes 786440 | tf_op jit(solution)/shard_map/ppermute | solution.py:50
  13.1 0.3 collective-permute-done.3
  13.4 1.3 %collective-permute-start.4 = (bf16[64,1024]{1,0:T(8,128)(2,1)S(1)}, bf16[64,1024]{1,0:T(8,128)(2,1)S(1)}, u32[]{:S(2)}, u32[]{:S(2)}) collective-permute-start(bf16[64,1024]{1,0:T(8,128)(2,1)S(1)} %select_select_fusion.2), channel_id=1, source_target_pairs={{0,96},{8,104},{1,97},{9,105},{2,98},{10,106},{3,99},{11,107},{16,... | collective-permute-start | bytes 393224 | tf_op jit(solution)/shard_map/ppermute | solution.py:70
  14.8 1.5 %collective-permute-start.5 = (bf16[64,1024]{1,0:T(8,128)(2,1)S(1)}, bf16[64,1024]{1,0:T(8,128)(2,1)S(1)}, u32[]{:S(2)}, u32[]{:S(2)}) collective-permute-start(bf16[64,1024]{1,0:T(8,128)(2,1)S(1)} %select_select_fusion.2), channel_id=1, source_target_pairs={{0,192},{8,200},{1,193},{9,201},{2,194},{10,202},{3,195},{11,203},... | collective-permute-start | bytes 393224 | tf_op jit(solution)/shard_map/ppermute | solution.py:70
  16.2 2.8 %collective-permute-done.6.near_ref = bf16[64,2048]{1,0:T(8,128)(2,1)S(1)} collective-permute-done((bf16[64,2048]{1,0:T(8,128)(2,1)S(1)}, bf16[64,2048]{1,0:T(8,128)(2,1)S(1)}, u32[]{:S(2)}, u32[]{:S(2)}) %collective-permute-start.6) | collective-permute-done | bytes 262176 | tf_op jit(solution)/shard_map/ppermute | solution.py:50
  19.1 0.7 %collective-permute-start.8 = (bf16[64,1024]{1,0:T(8,128)(2,1)S(1)}, bf16[64,1024]{1,0:T(8,128)(2,1)S(1)}, u32[]{:S(2)}, u32[]{:S(2)}) collective-permute-start(bf16[64,1024]{1,0:T(8,128)(2,1)S(1)} %select_select_fusion.1), channel_id=1, source_target_pairs={{96,64},{104,72},{97,65},{105,73},{98,66},{106,74},{99,67},{107,75... | collective-permute-start | bytes 393224 | tf_op jit(solution)/shard_map/ppermute | solution.py:70
  19.8 1.3 %collective-permute-start.9 = (bf16[64,1024]{1,0:T(8,128)(2,1)S(1)}, bf16[64,1024]{1,0:T(8,128)(2,1)S(1)}, u32[]{:S(2)}, u32[]{:S(2)}) collective-permute-start(bf16[64,1024]{1,0:T(8,128)(2,1)S(1)} %select_select_fusion.1), channel_id=1, source_target_pairs={{0,32},{8,40},{1,33},{9,41},{2,34},{10,42},{3,35},{11,43},{16,48},... | collective-permute-start | bytes 393224 | tf_op jit(solution)/shard_map/ppermute | solution.py:70
  21.3 2.7 %collective-permute-start.14 = (bf16[64,1024]{1,0:T(8,128)(2,1)S(1)}, bf16[64,1024]{1,0:T(8,128)(2,1)S(1)}, u32[]{:S(2)}, u32[]{:S(2)}) collective-permute-start(bf16[64,1024]{1,0:T(8,128)(2,1)S(1)} %slice.23), channel_id=1, source_target_pairs={{0,3},{8,11},{32,35},{40,43},{64,67},{72,75},{96,99},{104,107},{12... | collective-permute-start | bytes 393224 | tf_op jit(solution)/shard_map/ppermute | solution.py:50
  24.0 1.0 %collective-permute-start.10 = (bf16[64,1024]{1,0:T(8,128)(2,1)S(1)}, bf16[64,1024]{1,0:T(8,128)(2,1)S(1)}, u32[]{:S(2)}, u32[]{:S(2)}) collective-permute-start(bf16[64,1024]{1,0:T(8,128)(2,1)S(1)} %select_select_fusion.refs_0_), channel_id=1, source_target_pairs={{0,2},{8,10},{32,34},{40,42},{64,66},{72,74},{96,98},{104,106},{12... | collective-permute-start | bytes 393224 | tf_op jit(solution)/shard_map/ppermute | solution.py:50
  25.0 1.1 %collective-permute-start.11 = (bf16[64,1024]{1,0:T(8,128)(2,1)S(1)}, bf16[64,1024]{1,0:T(8,128)(2,1)S(1)}, u32[]{:S(2)}, u32[]{:S(2)}) collective-permute-start(bf16[64,1024]{1,0:T(8,128)(2,1)S(1)} %select_select_fusion.refs_0_), channel_id=1, source_target_pairs={{0,1},{8,9},{32,33},{40,41},{64,65},{72,73},{96,97},{104,105},{128... | collective-permute-start | bytes 393224 | tf_op jit(solution)/shard_map/ppermute | solution.py:50
  26.0 1.6 %collective-permute-start.12 = (bf16[64,1024]{1,0:T(8,128)(2,1)S(1)}, bf16[64,1024]{1,0:T(8,128)(2,1)S(1)}, u32[]{:S(2)}, u32[]{:S(2)}) collective-permute-start(bf16[64,1024]{1,0:T(8,128)(2,1)S(1)} %select_select_fusion.refs_0_), channel_id=1, source_target_pairs={{0,3},{8,11},{32,35},{40,43},{64,67},{72,75},{96,99},{104,107},{12... | collective-permute-start | bytes 393224 | tf_op jit(solution)/shard_map/ppermute | solution.py:50
  27.6 1.1 %own_attention.1.state_ref = f32[8,256,384]{2,1,0:T(8,128)S(1)} custom-call(bf16[64,4096]{1,0:T(8,128)(2,1)S(1)} %copy-done, bf16[64,2048]{1,0:T(8,128)(2,1)S(1)} %pad_maximum_fusion.1.own_ref, bf16[64,2048]{1,0:T(8,128)(2,1)S(1)} %collective-permute-done.6.near_ref, bf16[64,2048]{1,0:T(8,128)(2,1)S(1)} %collective-permute-done.7.far_ref, ...), custom_call_target="tpu_custom_call" | custom-call | flops 268435456 | bytes 4194304 | tf_op jit(solution)/shard_map/own_attention/pallas_call | solution.py:144
  28.8 2.3 %collective-permute-done.10.refs_1_ = bf16[64,1024]{1,0:T(8,128)(2,1)S(1)} collective-permute-done((bf16[64,1024]{1,0:T(8,128)(2,1)S(1)}, bf16[64,1024]{1,0:T(8,128)(2,1)S(1)}, u32[]{:S(2)}, u32[]{:S(2)}) %collective-permute-start.10) | collective-permute-done | bytes 131104 | tf_op jit(solution)/shard_map/ppermute | solution.py:50
  31.1 1.1 %collective-permute-done.11.refs_2_ = bf16[64,1024]{1,0:T(8,128)(2,1)S(1)} collective-permute-done((bf16[64,1024]{1,0:T(8,128)(2,1)S(1)}, bf16[64,1024]{1,0:T(8,128)(2,1)S(1)}, u32[]{:S(2)}, u32[]{:S(2)}) %collective-permute-start.11) | collective-permute-done | bytes 131104 | tf_op jit(solution)/shard_map/ppermute | solution.py:50
  32.3 2.4 %collective-permute-start.15 = (bf16[256,1024]{1,0:T(8,128)(2,1)S(1)}, bf16[256,1024]{1,0:T(8,128)(2,1)S(1)}, u32[]{:S(2)}, u32[]{:S(2)}) collective-permute-start(bf16[256,1024]{1,0:T(8,128)(2,1)S(1)} %pad_maximum_fusion), channel_id=1, source_target_pairs={{0,8},{8,0},{32,40},{40,32},{64,72},{72,64},{96,104},{104,96},{128... | collective-permute-start | bytes 1572872 | tf_op jit(solution)/shard_map/ppermute | solution.py:55
  34.7 1.5 %anchor_attention.2.refs_0_ = bf16[64,4096]{1,0:T(8,128)(2,1)} custom-call(bf16[64,4096]{1,0:T(8,128)(2,1)S(1)} %copy-done, f32[8,256,384]{2,1,0:T(8,128)S(1)} %own_attention.1.state_ref, bf16[64,1024]{1,0:T(8,128)(2,1)S(1)} %select_select_fusion.refs_0_, bf16[64,1024]{1,0:T(8,128)(2,1)S(1)} %collective-permute-done.10.refs_1_, ...), custom_call_target="tpu_custom_call" | custom-call | flops 134217728 | bytes 2097152 | tf_op jit(solution)/shard_map/anchor_attention/pallas_call | solution.py:193
  36.3 1.5 %anchor_attention.3 = bf16[64,4096]{1,0:T(8,128)(2,1)} custom-call(bf16[64,4096]{1,0:T(8,128)(2,1)S(1)} %copy-done, f32[8,256,384]{2,1,0:T(8,128)S(1)} %own_attention.1.state_ref, bf16[64,4096]{1,0:T(8,128)(2,1)} %anchor_attention.2.refs_0_, bf16[256,1024]{1,0:T(8,128)(2,1)S(1)} %collective-permute-done.15.refs_1_), custom_call_target="tpu_custom_call", output_to_operand_aliasing={{}: (2, {})} | custom-call | flops 134217728 | bytes 2097152 | tf_op jit(solution)/shard_map/anchor_attention/pallas_call | solution.py:193
  (23 shorter events, 0.5 us)
Async XLA Ops:
  0.0 27.6 %copy-start = (bf16[64,4096]{1,0:T(8,128)(2,1)S(1)}, bf16[64,4096]{1,0:T(8,128)(2,1)}, u32[]{:S(2)}) copy-start(bf16[64,4096]{1,0:T(8,128)(2,1)} %q_ref.5) | copy-start | bytes 1572868
  1.0 5.4 %collective-permute-start = (bf16[64,1024]{1,0:T(8,128)(2,1)S(1)}, bf16[64,1024]{1,0:T(8,128)(2,1)S(1)}, u32[]{:S(2)}, u32[]{:S(2)}) collective-permute-start(bf16[64,1024]{1,0:T(8,128)(2,1)S(1)} %pad_maximum_fusion.2), channel_id=1, source_target_pairs={{0,8},{1,9},{2,10},{3,11}} | collective-permute-start | bytes 393224 | tf_op jit(solution)/shard_map/ppermute | solution.py:220
  6.4 6.7 %collective-permute-start.1 = (bf16[64,1024]{1,0:T(8,128)(2,1)S(1)}, bf16[64,1024]{1,0:T(8,128)(2,1)S(1)}, u32[]{:S(2)}, u32[]{:S(2)}) collective-permute-start(bf16[64,1024]{1,0:T(8,128)(2,1)S(1)} %maximum_select_fusion), channel_id=1, source_target_pairs={{0,4},{8,12},{1,5},{9,13},{2,6},{10,14},{3,7},{11,15}} | collective-permute-start | bytes 393224 | tf_op jit(solution)/shard_map/ppermute | solution.py:70
  7.7 5.4 %collective-permute-start.2 = (bf16[64,1024]{1,0:T(8,128)(2,1)S(1)}, bf16[64,1024]{1,0:T(8,128)(2,1)S(1)}, u32[]{:S(2)}, u32[]{:S(2)}) collective-permute-start(bf16[64,1024]{1,0:T(8,128)(2,1)S(1)} %maximum_select_fusion), channel_id=1, source_target_pairs={{0,20},{8,28},{1,21},{9,29},{2,22},{10,30},{3,23},{11,31}} | collective-permute-start | bytes 393224 | tf_op jit(solution)/shard_map/ppermute | solution.py:70
  9.0 4.4 %collective-permute-start.3 = (bf16[64,1024]{1,0:T(8,128)(2,1)S(1)}, bf16[64,1024]{1,0:T(8,128)(2,1)S(1)}, u32[]{:S(2)}, u32[]{:S(2)}) collective-permute-start(bf16[64,1024]{1,0:T(8,128)(2,1)S(1)} %maximum_select_fusion), channel_id=1, source_target_pairs={{0,16},{8,24},{1,17},{9,25},{2,18},{10,26},{3,19},{11,27}} | collective-permute-start | bytes 393224 | tf_op jit(solution)/shard_map/ppermute | solution.py:70
  10.4 8.7 %collective-permute-start.6 = (bf16[64,2048]{1,0:T(8,128)(2,1)S(1)}, bf16[64,2048]{1,0:T(8,128)(2,1)S(1)}, u32[]{:S(2)}, u32[]{:S(2)}) collective-permute-start(bf16[64,2048]{1,0:T(8,128)(2,1)S(1)} %pad_maximum_fusion.1.own_ref), channel_id=1, source_target_pairs={{0,1},{8,9},{32,33},{40,41},{64,65},{72,73},{96,97},{104,105},{128... | collective-permute-start | bytes 786440 | tf_op jit(solution)/shard_map/ppermute | solution.py:50
  11.3 7.8 %collective-permute-start.7 = (bf16[64,2048]{1,0:T(8,128)(2,1)S(1)}, bf16[64,2048]{1,0:T(8,128)(2,1)S(1)}, u32[]{:S(2)}, u32[]{:S(2)}) collective-permute-start(bf16[64,2048]{1,0:T(8,128)(2,1)S(1)} %pad_maximum_fusion.1.own_ref), channel_id=1, source_target_pairs={{0,3},{8,11},{32,35},{40,43},{64,67},{72,75},{96,99},{104,107},{12... | collective-permute-start | bytes 786440 | tf_op jit(solution)/shard_map/ppermute | solution.py:50
  13.4 5.6 %collective-permute-start.4 = (bf16[64,1024]{1,0:T(8,128)(2,1)S(1)}, bf16[64,1024]{1,0:T(8,128)(2,1)S(1)}, u32[]{:S(2)}, u32[]{:S(2)}) collective-permute-start(bf16[64,1024]{1,0:T(8,128)(2,1)S(1)} %select_select_fusion.2), channel_id=1, source_target_pairs={{0,96},{8,104},{1,97},{9,105},{2,98},{10,106},{3,99},{11,107},{16,... | collective-permute-start | bytes 393224 | tf_op jit(solution)/shard_map/ppermute | solution.py:70
  14.8 4.3 %collective-permute-start.5 = (bf16[64,1024]{1,0:T(8,128)(2,1)S(1)}, bf16[64,1024]{1,0:T(8,128)(2,1)S(1)}, u32[]{:S(2)}, u32[]{:S(2)}) collective-permute-start(bf16[64,1024]{1,0:T(8,128)(2,1)S(1)} %select_select_fusion.2), channel_id=1, source_target_pairs={{0,192},{8,200},{1,193},{9,201},{2,194},{10,202},{3,195},{11,203},... | collective-permute-start | bytes 393224 | tf_op jit(solution)/shard_map/ppermute | solution.py:70
  19.1 4.9 %collective-permute-start.8 = (bf16[64,1024]{1,0:T(8,128)(2,1)S(1)}, bf16[64,1024]{1,0:T(8,128)(2,1)S(1)}, u32[]{:S(2)}, u32[]{:S(2)}) collective-permute-start(bf16[64,1024]{1,0:T(8,128)(2,1)S(1)} %select_select_fusion.1), channel_id=1, source_target_pairs={{96,64},{104,72},{97,65},{105,73},{98,66},{106,74},{99,67},{107,75... | collective-permute-start | bytes 393224 | tf_op jit(solution)/shard_map/ppermute | solution.py:70
  19.8 4.2 %collective-permute-start.9 = (bf16[64,1024]{1,0:T(8,128)(2,1)S(1)}, bf16[64,1024]{1,0:T(8,128)(2,1)S(1)}, u32[]{:S(2)}, u32[]{:S(2)}) collective-permute-start(bf16[64,1024]{1,0:T(8,128)(2,1)S(1)} %select_select_fusion.1), channel_id=1, source_target_pairs={{0,32},{8,40},{1,33},{9,41},{2,34},{10,42},{3,35},{11,43},{16,48},... | collective-permute-start | bytes 393224 | tf_op jit(solution)/shard_map/ppermute | solution.py:70
  21.1 6.5 %collective-permute-start.13 = (bf16[64,1024]{1,0:T(8,128)(2,1)S(1)}, bf16[64,1024]{1,0:T(8,128)(2,1)S(1)}, u32[]{:S(2)}, u32[]{:S(2)}) collective-permute-start(bf16[64,1024]{1,0:T(8,128)(2,1)S(1)} %slice.22), channel_id=1, source_target_pairs={{0,1},{8,9},{32,33},{40,41},{64,65},{72,73},{96,97},{104,105},{128... | collective-permute-start | bytes 393224 | tf_op jit(solution)/shard_map/ppermute | solution.py:50
  21.3 6.4 %collective-permute-start.14 = (bf16[64,1024]{1,0:T(8,128)(2,1)S(1)}, bf16[64,1024]{1,0:T(8,128)(2,1)S(1)}, u32[]{:S(2)}, u32[]{:S(2)}) collective-permute-start(bf16[64,1024]{1,0:T(8,128)(2,1)S(1)} %slice.23), channel_id=1, source_target_pairs={{0,3},{8,11},{32,35},{40,43},{64,67},{72,75},{96,99},{104,107},{12... | collective-permute-start | bytes 393224 | tf_op jit(solution)/shard_map/ppermute | solution.py:50
  24.0 7.1 %collective-permute-start.10 = (bf16[64,1024]{1,0:T(8,128)(2,1)S(1)}, bf16[64,1024]{1,0:T(8,128)(2,1)S(1)}, u32[]{:S(2)}, u32[]{:S(2)}) collective-permute-start(bf16[64,1024]{1,0:T(8,128)(2,1)S(1)} %select_select_fusion.refs_0_), channel_id=1, source_target_pairs={{0,2},{8,10},{32,34},{40,42},{64,66},{72,74},{96,98},{104,106},{12... | collective-permute-start | bytes 393224 | tf_op jit(solution)/shard_map/ppermute | solution.py:50
  25.0 7.2 %collective-permute-start.11 = (bf16[64,1024]{1,0:T(8,128)(2,1)S(1)}, bf16[64,1024]{1,0:T(8,128)(2,1)S(1)}, u32[]{:S(2)}, u32[]{:S(2)}) collective-permute-start(bf16[64,1024]{1,0:T(8,128)(2,1)S(1)} %select_select_fusion.refs_0_), channel_id=1, source_target_pairs={{0,1},{8,9},{32,33},{40,41},{64,65},{72,73},{96,97},{104,105},{128... | collective-permute-start | bytes 393224 | tf_op jit(solution)/shard_map/ppermute | solution.py:50
  26.0 6.3 %collective-permute-start.12 = (bf16[64,1024]{1,0:T(8,128)(2,1)S(1)}, bf16[64,1024]{1,0:T(8,128)(2,1)S(1)}, u32[]{:S(2)}, u32[]{:S(2)}) collective-permute-start(bf16[64,1024]{1,0:T(8,128)(2,1)S(1)} %select_select_fusion.refs_0_), channel_id=1, source_target_pairs={{0,3},{8,11},{32,35},{40,43},{64,67},{72,75},{96,99},{104,107},{12... | collective-permute-start | bytes 393224 | tf_op jit(solution)/shard_map/ppermute | solution.py:50
  32.3 3.9 %collective-permute-start.15 = (bf16[256,1024]{1,0:T(8,128)(2,1)S(1)}, bf16[256,1024]{1,0:T(8,128)(2,1)S(1)}, u32[]{:S(2)}, u32[]{:S(2)}) collective-permute-start(bf16[256,1024]{1,0:T(8,128)(2,1)S(1)} %pad_maximum_fusion), channel_id=1, source_target_pairs={{0,8},{8,0},{32,40},{40,32},{64,72},{72,64},{96,104},{104,96},{128... | collective-permute-start | bytes 1572872 | tf_op jit(solution)/shard_map/ppermute | solution.py:55
